TPU v7x, 32 devices: a whole 2x2x4 slice. The times are simulated.
32 devices in a mesh: dp: 4 (over y, core), seq: 8 (over z, x).
Axes of the slice: x: 2, y: 2, z: 4, core: 2. Of those that a mesh axis runs over, the one named last changes fastest.
Arguments:
- region: bfloat16 [32, 512, 192], P(('dp', 'seq')), parts along dimension 0, may hold values from -11 to 11
- norm_gain: float32 [192], replicated, may hold values from 0.1 to 1.9
- in_weight: bfloat16 [192, 768], replicated, may hold values from -0.4375 to 0.4375
- conv_weight: float32 [9, 384], replicated, may hold values from -2 to 2
- conv_bias: float32 [384], replicated, may hold values from -3 to 3
- coupling_weight: bfloat16 [384, 512], replicated, may hold values from -0.3125 to 0.3125
- step_weight: bfloat16 [384, 24], replicated, may hold values from -0.3125 to 0.3125
- step_bias: float32 [24], replicated, may hold values from -1 to 1
- decay_log: float32 [24], replicated, may hold values from -16 to -2.9
- skip_gain: float32 [24], replicated, may hold values from 0.5 to 12
- out_gain: float32 [384], replicated, may hold values from 0.1 to 1.9
- out_weight: bfloat16 [384, 192], replicated, may hold values from -0.3125 to 0.3125
Outputs:
- refined: bfloat16 [32, 512, 192], P(('dp', 'seq')), parts along dimension 0
There are 4 independent parts, one for each index of `dp`. A program takes and returns all parts, laid end to end along the dimension named above; an argument that names none is the same for every part. Nothing has to cross between parts.
All inputs are finite; a program needn't handle non-finite values.
Results may differ from a plain program's by a relative error of at most 0.0035.
The roundings to bfloat16 on the way count: a program that leaves them out, or rounds other values in their place, can miss the bound.
Values may be sent and summed in bfloat16 or wider, within the bound.
A program may use at most 128 MiB of HBM per device.

v0:
```python
import jax
import jax.numpy as jnp
from jax import lax
from jax.sharding import PartitionSpec as P

BLOCK = 512


EPSILON = 1e-05


def with_halo(block, sides, width):
    for axis, dim in sides:
        count = lax.axis_size(axis)
        forward = [(i, i + 1) for i in range(count - 1)]
        backward = [(target, source) for source, target in forward]
        low = lax.ppermute(
            lax.slice_in_dim(block, block.shape[dim] - width, None, axis=dim), axis, forward
        )
        high = lax.ppermute(lax.slice_in_dim(block, 0, width, axis=dim), axis, backward)
        block = jnp.concatenate([low, block, high], axis=dim)
    return block


def rms_scale(values, gain):
    mean_square = jnp.mean(values * values, axis=-1, keepdims=True)
    return values * lax.rsqrt(mean_square + EPSILON) * gain


def depthwise(padded, row_count, col_count, conv_weight, conv_bias):
    summed = conv_bias
    for offset_row in range(3):
        for offset_col in range(3):
            summed = (
                summed
                + padded[offset_row : offset_row + row_count, offset_col : offset_col + col_count]
                * conv_weight[offset_row * 3 + offset_col]
            )
    return jax.nn.silu(summed).astype(jnp.bfloat16)


def block_local(signal, writer, reader, log_decay, step_sizes, skip_part):
    seq_length, inner_width = signal.shape
    head_count = log_decay.shape[1]
    head_size = inner_width // head_count
    block_count = seq_length // BLOCK
    value_blocks = signal.reshape(block_count, BLOCK, head_count, head_size)
    writer_blocks = writer.reshape(block_count, BLOCK, -1)
    reader_blocks = reader.reshape(block_count, BLOCK, -1)
    step_blocks = step_sizes.reshape(block_count, BLOCK, head_count)
    cumul = jnp.cumsum(log_decay.reshape(block_count, BLOCK, head_count), axis=1)
    causal = lax.broadcasted_iota(jnp.int32, (BLOCK, BLOCK), 0) >= lax.broadcasted_iota(
        jnp.int32, (BLOCK, BLOCK), 1
    )

    def one_block(pieces):
        value_part, writer_part, reader_part, cumul_part, step_part = pieces
        scores = jnp.dot(reader_part, writer_part.T, preferred_element_type=jnp.float32)
        cum_heads = cumul_part.T
        spread = jnp.where(causal[None], cum_heads[:, :, None] - cum_heads[:, None, :], -jnp.inf)
        mixing = (scores[None] * jnp.exp(spread) * step_part.T[:, None, :]).astype(jnp.bfloat16)
        inside = jnp.einsum("hts,shp->thp", mixing, value_part, preferred_element_type=jnp.float32)
        tail_weight = jnp.exp(cumul_part[-1][None, :] - cumul_part) * step_part
        weighted = (value_part * tail_weight[:, :, None]).astype(jnp.bfloat16)
        contrib = jnp.einsum(
            "shp,sn->hpn", weighted, writer_part, preferred_element_type=jnp.float32
        )
        return (inside, contrib)

    inside, contrib = lax.map(
        one_block, (value_blocks, writer_blocks, reader_blocks, cumul, step_blocks)
    )
    decays = cumul[:, -1, :]

    def advance(carried, pieces):
        decay_now, added = pieces
        return (jnp.exp(decay_now)[:, None, None] * carried + added, carried)

    zero_state = jnp.zeros(contrib.shape[1:], jnp.float32)
    closing, starts = lax.scan(advance, zero_state, (decays, contrib))
    before = jnp.cumsum(decays, axis=0) - decays
    own_part = inside + value_blocks.astype(jnp.float32) * skip_part[None, None, :, None]
    return ((own_part, starts, before, cumul, reader_blocks), jnp.sum(decays, axis=0), closing)


def finish(local_terms, carried_in):
    own_part, starts, before, cumul, reader_blocks = local_terms
    entry_state = starts + jnp.exp(before)[:, :, None, None] * carried_in[None]
    entry_half = entry_state.astype(jnp.bfloat16)
    outer_part = jnp.einsum(
        "ktn,khpn->kthp", reader_blocks, entry_half, preferred_element_type=jnp.float32
    )
    result = own_part + outer_part * jnp.exp(cumul)[:, :, :, None]
    return result.reshape(-1, result.shape[2] * result.shape[3])


def carries(ahead_log, ahead_state, behind_log, behind_state):
    total_logs = jnp.stack([ahead_log, behind_log])[None]
    total_states = jnp.stack([ahead_state, behind_state])[None]
    all_logs, all_states = (
        lax.all_gather(total_logs, "seq", axis=0, tiled=True),
        lax.all_gather(total_states, "seq", axis=0, tiled=True),
    )
    own_index = lax.axis_index("seq")
    device_order = jnp.arange(all_logs.shape[0])
    running = jnp.cumsum(all_logs, axis=0)
    exclusive = running - all_logs
    ahead_mask = (device_order < own_index)[:, None]
    ahead_weight = jnp.exp(
        jnp.where(ahead_mask, exclusive[own_index, 0][None, :] - running[:, 0], -jnp.inf)
    )
    ahead_carry = jnp.sum(ahead_weight[:, :, None, None] * all_states[:, 0], axis=0)
    behind_mask = (device_order > own_index)[:, None]
    behind_weight = jnp.exp(
        jnp.where(behind_mask, exclusive[:, 1] - running[own_index, 1][None, :], -jnp.inf)
    )
    behind_carry = jnp.sum(behind_weight[:, :, None, None] * all_states[:, 1], axis=0)
    return (ahead_carry, behind_carry)


def order_pair(signal, coupling_part, step_sizes, decay_rates, skip_pair, head_count, state_size):
    ahead_terms = block_local(
        signal,
        coupling_part[:, :state_size],
        coupling_part[:, state_size : 2 * state_size],
        -decay_rates[:head_count] * step_sizes[:, :head_count],
        step_sizes[:, :head_count],
        skip_pair[:head_count],
    )
    behind_steps = jnp.flip(step_sizes[:, head_count:], 0)
    behind_terms = block_local(
        jnp.flip(signal, 0),
        jnp.flip(coupling_part[:, 2 * state_size : 3 * state_size], 0),
        jnp.flip(coupling_part[:, 3 * state_size :], 0),
        -decay_rates[head_count:] * behind_steps,
        behind_steps,
        skip_pair[head_count:],
    )
    ahead_carry, behind_carry = carries(
        ahead_terms[1], ahead_terms[2], behind_terms[1], behind_terms[2]
    )
    ahead_out = finish(ahead_terms[0], ahead_carry)
    behind_out = jnp.flip(finish(behind_terms[0], behind_carry), 0)
    return ahead_out + behind_out


def body(
    region,
    norm_gain,
    in_weight,
    conv_weight,
    conv_bias,
    coupling_weight,
    step_weight,
    step_bias,
    decay_log,
    skip_gain,
    out_gain,
    out_weight,
):
    row_count, col_count, feat_width = region.shape
    inner_width = in_weight.shape[1] // 2
    head_count = step_bias.shape[0] // 4
    state_size = coupling_weight.shape[1] // 8
    token_count = row_count * col_count
    flat_region = region.reshape(token_count, feat_width).astype(jnp.float32)
    normed = rms_scale(flat_region, norm_gain).astype(jnp.bfloat16)
    projected = jnp.dot(normed, in_weight, preferred_element_type=jnp.float32).astype(jnp.bfloat16)
    pre_conv = projected[:, :inner_width].reshape(row_count, col_count, inner_width)
    gate_part = projected[:, inner_width:]
    rimmed = with_halo(pre_conv, (("seq", 0),), 1)
    padded = jnp.pad(rimmed, ((0, 0), (1, 1), (0, 0)))
    activated = depthwise(padded, row_count, col_count, conv_weight, conv_bias)
    row_inputs = activated.reshape(token_count, inner_width)
    decay_rates = jnp.exp(decay_log)
    half_width = 4 * state_size
    coupling_every = jnp.dot(
        row_inputs, coupling_weight, preferred_element_type=jnp.float32
    ).astype(jnp.bfloat16)
    coupling_rows = coupling_every[:, :half_width]
    coupling_send = coupling_every[:, half_width:].reshape(row_count, col_count, half_width)
    moved_inputs, coupling_moved = (
        lax.all_to_all(activated, "seq", split_axis=1, concat_axis=0, tiled=True),
        lax.all_to_all(coupling_send, "seq", split_axis=1, concat_axis=0, tiled=True),
    )
    step_rows = jax.nn.softplus(
        jnp.dot(row_inputs, step_weight[:, : 2 * head_count], preferred_element_type=jnp.float32)
        + step_bias[: 2 * head_count]
    )
    row_total = order_pair(
        row_inputs,
        coupling_rows,
        step_rows,
        decay_rates[: 2 * head_count],
        skip_gain[: 2 * head_count],
        head_count,
        state_size,
    )
    band_rows = moved_inputs.shape[0]
    band_cols = moved_inputs.shape[1]
    column_inputs = jnp.transpose(moved_inputs, (1, 0, 2)).reshape(token_count, inner_width)
    coupling_cols = jnp.transpose(coupling_moved, (1, 0, 2)).reshape(token_count, half_width)
    step_cols = jax.nn.softplus(
        jnp.dot(column_inputs, step_weight[:, 2 * head_count :], preferred_element_type=jnp.float32)
        + step_bias[2 * head_count :]
    )
    column_sum = order_pair(
        column_inputs,
        coupling_cols,
        step_cols,
        decay_rates[2 * head_count :],
        skip_gain[2 * head_count :],
        head_count,
        state_size,
    )
    column_half = column_sum.astype(jnp.bfloat16)
    column_grid = jnp.transpose(column_half.reshape(band_cols, band_rows, inner_width), (1, 0, 2))
    col_total = lax.all_to_all(column_grid, "seq", split_axis=0, concat_axis=1, tiled=True).reshape(
        token_count, inner_width
    )
    combined = row_total + col_total.astype(jnp.float32)
    gated = combined * jax.nn.silu(gate_part.astype(jnp.float32))
    normy = rms_scale(gated, out_gain).astype(jnp.bfloat16)
    refined = flat_region + jnp.dot(normy, out_weight, preferred_element_type=jnp.float32)
    return refined.astype(jnp.bfloat16).reshape(row_count, col_count, feat_width)


def solution(mesh):
    in_specs = (P(("dp", "seq"), None, None), P(), P(), P(), P(), P(), P(), P(), P(), P(), P(), P())
    out_specs = P(("dp", "seq"), None, None)
    return jax.shard_map(body, mesh=mesh, in_specs=in_specs, out_specs=out_specs, check_vma=False)
```

profile of v0, /device:TPU:0, one launch (start us, length us, event | category | flops | bytes accessed | tf_op | source)
XLA Modules:
  0.0 244.7 jit_solution(17092413996549923992)
XLA Ops:
  6.5 1.1 fusion.52
  7.6 1.6 convolution_convert_fusion
  9.2 1.3 collective-permute-start.1
  10.5 5.5 %collective-permute-start = (bf16[1,512,384]{2,1,0:T(8,128)(2,1)S(1)}, bf16[1,512,384]{2,1,0:T(8,128)(2,1)S(1)}, u32[]{:S(2)}, u32[]{:S(2)}) collective-permute-start(bf16[1,512,384]{2,1,0:T(8,128)(2,1)S(1)} %slice_bitcast_fusion.4), channel_id=1, source_target_pairs={{0,1},{1,2},{2,3},{3,4},{4,5},{5,6},{6,7},{8,9},{9,10},{10,11},{11... | collective-permute-start | bytes 1179656 | tf_op jit(solution)/shard_map/ppermute | solution.py:17
  16.0 1.0 slice_reduce_fusion.12
  17.1 1.3 fusion.142
  21.1 1.4 fusion.141
  23.2 8.6 %collective-permute-done = bf16[1,512,384]{2,1,0:T(8,128)(2,1)S(1)} collective-permute-done((bf16[1,512,384]{2,1,0:T(8,128)(2,1)S(1)}, bf16[1,512,384]{2,1,0:T(8,128)(2,1)S(1)}, u32[]{:S(2)}, u32[]{:S(2)}) %collective-permute-start) | collective-permute-done | bytes 393248 | tf_op jit(solution)/shard_map/ppermute | solution.py:17
  32.1 0.9 multiply_convert_fusion.25
  33.5 1.8 reduce-window.26
  37.5 1.3 fusion.88
  41.1 2.1 reduce.31
  44.0 5.8 %all-to-all-start.1 = ((bf16[8,2,8192]{2,1,0:T(2,128)(2,1)}), bf16[8,2,8192]{2,1,0:T(2,128)(2,1)S(1)}, u32[]{:S(2)}, u32[]{:S(2)}) async-start(bf16[8,2,8192]{2,1,0:T(2,128)(2,1)} %reshape.748), calls=%async_computation.1 | async-start | bytes 524288 | tf_op jit(solution)/shard_map/all_to_all | solution.py:184
  50.5 1.3 fusion.143
  51.8 0.9 fusion.39
  53.4 2.9 %reduce.30 = bf16[512,384]{1,0:T(8,128)(2,1)S(1)} reduce(bf16[512,1,384]{2,1,0:T(2,128)(2,1)S(1)} %bitcast.315, bf16[]{:T(256)} %broadcast.311), dimensions={1}, to_apply=%bitcast.302.reduce_sub_computation | reduce | bytes 786434
  57.2 1.4 rev.34
  59.1 0.9 copy.110
  60.0 4.4 %fusion.28 = f32[512,6,64]{0,2,1:T(8,128)} fusion(bf16[512,6,64]{0,2,1:T(8,128)(2,1)} %bitcast.327, f32[6,512]{1,0:T(8,128)} %get-tuple-element.173, f32[6,512]{1,0:T(8,128)} %fusion.118, f32[512,512]{1,0:T(8,128)} %fusion.88, pred[512,512]{1,0:T(8,128)(4,1)} %iota_compare_fusion.2, f32[6]{0:T(128)} %get-tuple-element.190), kind=kOutput, calls=%fused_computation.44 | convolution fusion | flops 209780736 | bytes 2514968 | tf_op jit(solution)/shard_map/while/body/eval_jaxpr/hts,shp->thp/dot_general | solution.py:62
  64.5 6.0 %all-to-all-start = ((bf16[8,2,12288]{2,1,0:T(2,128)(2,1)}), bf16[8,2,12288]{2,1,0:T(2,128)(2,1)S(1)}, u32[]{:S(2)}, u32[]{:S(2)}) async-start(bf16[8,2,12288]{2,1,0:T(2,128)(2,1)} %reshape.746), calls=%async_computation | async-start | bytes 786432 | tf_op jit(solution)/shard_map/all_to_all | solution.py:183
  71.7 1.4 fusion.74
  73.1 1.3 fusion.144
  74.4 7.4 %all-to-all-done = bf16[8,2,12288]{2,1,0:T(2,128)(2,1)S(1)} async-done(((bf16[8,2,12288]{2,1,0:T(2,128)(2,1)}), bf16[8,2,12288]{2,1,0:T(2,128)(2,1)S(1)}, u32[]{:S(2)}, u32[]{:S(2)}) %all-to-all-start) | async-done | bytes 393248 | tf_op jit(solution)/shard_map/all_to_all | solution.py:183
  82.5 1.1 compare_select_fusion
  83.7 1.8 reduce-window.34
  88.4 1.8 reduce-window.36
  93.9 1.4 copy.124
  96.0 1.2 fusion.36
  97.2 1.3 fusion.37
  99.4 1.8 reduce-window.30
  102.5 18.6 %all-gather.4 = f32[8,2,6]{2,1,0:T(2,128)S(1)} all-gather(f32[1,2,6]{2,1,0:T(2,128)S(1)} %maximum_bitcast_fusion), channel_id=2, replica_groups=mesh['dp'=4,'seq'=8] {'seq'}, dimensions={0}, use_global_device_ids=true | all-gather | bytes 432 | tf_op jit(solution)/shard_map/all_gather | solution.py:101
  121.2 16.5 %all-gather.5 = f32[8,2,6]{2,1,0:T(2,128)S(1)} all-gather(f32[1,2,6]{2,1,0:T(2,128)S(1)} %maximum_bitcast_fusion.1), channel_id=4, replica_groups=mesh['dp'=4,'seq'=8] {'seq'}, dimensions={0}, use_global_device_ids=true | all-gather | bytes 432 | tf_op jit(solution)/shard_map/all_gather | solution.py:101
  142.2 4.3 %fusion.30 = f32[512,6,64]{0,2,1:T(8,128)} fusion(bf16[512,6,64]{0,2,1:T(8,128)(2,1)} %copy.124, f32[6,512]{1,0:T(8,128)} %get-tuple-element.176, f32[6,512]{1,0:T(8,128)} %fusion.122, f32[512,512]{1,0:T(8,128)} %fusion.74, pred[512,512]{1,0:T(8,128)(4,1)} %iota_compare_fusion.2, f32[6]{0:T(128)} %get-tuple-element.192), kind=kOutput, calls=%fused_computation.46 | convolution fusion | flops 209780736 | bytes 2514968 | tf_op jit(solution)/shard_map/while/body/eval_jaxpr/hts,shp->thp/dot_general | solution.py:62
  146.6 2.9 %fusion.31 = f32[512,6,64]{0,2,1:T(8,128)} fusion(bf16[512,6,64]{0,2,1:T(8,128)(2,1)S(1)} %bitcast.320, f32[6,512]{1,0:T(8,128)S(1)} %bitcast.341, f32[6,512]{1,0:T(8,128)S(1)} %copy-done.32, f32[512,512]{1,0:T(8,128)S(1)} %copy-done.3, pred[512,512]{1,0:T(8,128)(4,1)S(1)} %copy-done.16, f32[6]{0:T(128)S(1)} %copy-done.51), kind=kOutput, calls=%fused_computation.47 | convolution fusion | flops 209780736 | bytes 2514968 | tf_op jit(solution)/shard_map/while/body/eval_jaxpr/hts,shp->thp/dot_general | solution.py:62
  149.6 3.0 %fusion.29 = f32[512,6,64]{0,2,1:T(8,128)} fusion(bf16[512,6,64]{0,2,1:T(8,128)(2,1)S(1)} %bitcast.325, f32[6,512]{1,0:T(8,128)S(1)} %bitcast.340, f32[6,512]{1,0:T(8,128)S(1)} %fusion.120, f32[512,512]{1,0:T(8,128)S(1)} %copy-done.4, pred[512,512]{1,0:T(8,128)(4,1)S(1)} %copy-done.16, f32[6]{0:T(128)S(1)} %copy-done.50), kind=kOutput, calls=%fused_computation.45 | convolution fusion | flops 209780736 | bytes 2514968 | tf_op jit(solution)/shard_map/while/body/eval_jaxpr/hts,shp->thp/dot_general | solution.py:62
  152.6 6.6 %all-gather.11.cloned.1.call-done = f32[16,6,64,64]{3,2,1,0:T(8,128)} async-done(((f32[2,6,64,64]{3,2,1,0:T(8,128)}), f32[16,6,64,64]{3,2,1,0:T(8,128)}) %all-gather.11.cloned.1.call-update) | async-done | bytes 1572880 | tf_op jit(solution)/shard_map/all_gather | solution.py:102
  159.2 2.4 fusion.10
  161.9 1.2 copy.136
  163.1 1.4 fusion.24
  165.2 1.2 fusion.55
  167.3 4.2 %all-to-all-start.2 = ((bf16[8,64,384]{2,1,0:T(8,128)(2,1)}), bf16[8,64,384]{2,1,0:T(8,128)(2,1)}, u32[]{:S(2)}, u32[]{:S(2)}) async-start(bf16[8,64,384]{2,1,0:T(8,128)(2,1)} %copy.137), calls=%async_computation.2 | async-start | bytes 786432 | tf_op jit(solution)/shard_map/all_to_all | solution.py:218
  171.5 57.1 %all-gather.9.cloned.1.call-done = f32[16,6,64,64]{3,2,1,0:T(8,128)} async-done(((f32[2,6,64,64]{3,2,1,0:T(8,128)}), f32[16,6,64,64]{3,2,1,0:T(8,128)}) %all-gather.9.cloned.1.call-update) | async-done | bytes 1572880 | tf_op jit(solution)/shard_map/all_gather | solution.py:102
  228.6 2.3 fusion.14
  231.0 0.9 fusion.27
  231.9 1.1 copy.112
  233.0 1.4 fusion.26
  235.1 1.6 multiply_reduce_fusion
  236.8 1.1 fusion.35
  (223 shorter events, 30.0 us)
Async XLA Ops:
  6.5 30.5 %copy-start = (bf16[384,512]{1,0:T(8,128)(2,1)S(1)}, bf16[384,512]{1,0:T(8,128)(2,1)}, u32[]{:S(2)}) copy-start(bf16[384,512]{1,0:T(8,128)(2,1)} %param.17) | copy-start | bytes 1179652
  6.5 25.5 %copy-start.40 = (f32[384]{0:T(512)S(1)}, f32[384]{0:T(512)}, u32[]{:S(2)}) copy-start(f32[384]{0:T(512)} %param.16) | copy-start | bytes 4612
  9.2 14.0 %collective-permute-start.1 = (bf16[1,512,384]{2,1,0:T(8,128)(2,1)S(1)}, bf16[1,512,384]{2,1,0:T(8,128)(2,1)S(1)}, u32[]{:S(2)}, u32[]{:S(2)}) collective-permute-start(bf16[1,512,384]{2,1,0:T(8,128)(2,1)S(1)} %slice_bitcast_fusion.4), channel_id=1, source_target_pairs={{1,0},{2,1},{3,2},{4,3},{5,4},{6,5},{7,6},{9,8},{10,9},{11,10},{12... | collective-permute-start | bytes 1179656 | tf_op jit(solution)/shard_map/ppermute | solution.py:20
  10.5 21.2 %collective-permute-start = (bf16[1,512,384]{2,1,0:T(8,128)(2,1)S(1)}, bf16[1,512,384]{2,1,0:T(8,128)(2,1)S(1)}, u32[]{:S(2)}, u32[]{:S(2)}) collective-permute-start(bf16[1,512,384]{2,1,0:T(8,128)(2,1)S(1)} %slice_bitcast_fusion.4), channel_id=1, source_target_pairs={{0,1},{1,2},{2,3},{3,4},{4,5},{5,6},{6,7},{8,9},{9,10},{10,11},{11... | collective-permute-start | bytes 1179656 | tf_op jit(solution)/shard_map/ppermute | solution.py:17
  22.5 10.7 %copy-start.33 = (bf16[384,24]{0,1:T(8,128)(2,1)S(1)}, bf16[384,24]{0,1:T(8,128)(2,1)}, u32[]{:S(2)}) copy-start(bf16[384,24]{0,1:T(8,128)(2,1)} %param.18) | copy-start | bytes 55300
  33.2 18.6 %copy-start.11 = (bf16[1,512,384]{1,2,0:T(8,128)(2,1)}, bf16[1,512,384]{1,2,0:T(8,128)(2,1)S(1)}, u32[]{:S(2)}) copy-start(bf16[1,512,384]{1,2,0:T(8,128)(2,1)S(1)} %copy.99) | copy-start | bytes 1179652
  39.0 10.8 %copy-start.34 = (f32[6]{0:T(128)}, f32[6]{0:T(128)S(1)}, u32[]{:S(2)}) copy-start(f32[6]{0:T(128)S(1)} %slice_reduce_fusion.3) | copy-start | bytes 76
  44.0 20.5 %all-to-all-start.1 = ((bf16[8,2,8192]{2,1,0:T(2,128)(2,1)}), bf16[8,2,8192]{2,1,0:T(2,128)(2,1)S(1)}, u32[]{:S(2)}, u32[]{:S(2)}) async-start(bf16[8,2,8192]{2,1,0:T(2,128)(2,1)} %reshape.748), calls=%async_computation.1 | async-start | bytes 524288 | tf_op jit(solution)/shard_map/all_to_all | solution.py:184
  50.1 3.2 %copy-start.14 = (bf16[512,64]{0,1:T(8,128)(2,1)}, bf16[512,64]{0,1:T(8,128)(2,1)S(1)}, u32[]{:S(2)}) copy-start(bf16[512,64]{0,1:T(8,128)(2,1)S(1)} %rev.36) | copy-start | bytes 196612
  64.5 17.3 %all-to-all-start = ((bf16[8,2,12288]{2,1,0:T(2,128)(2,1)}), bf16[8,2,12288]{2,1,0:T(2,128)(2,1)S(1)}, u32[]{:S(2)}, u32[]{:S(2)}) async-start(bf16[8,2,12288]{2,1,0:T(2,128)(2,1)} %reshape.746), calls=%async_computation | async-start | bytes 786432 | tf_op jit(solution)/shard_map/all_to_all | solution.py:183
  70.5 88.7 %all-gather.11.cloned.1.call-start = ((), (), s32[]{:S(2)}) async-start(), calls=%async_computation.4 | async-start | bytes 3538944 | tf_op jit(solution)/shard_map/all_gather | solution.py:102
  71.3 11.2 %copy-start.49 = (f32[12]{0:T(128)S(1)}, f32[12]{0:T(128)}, u32[]{:S(2)}) copy-start(f32[12]{0:T(128)} %get-tuple-element.218) | copy-start | bytes 148
  71.5 12.1 %copy-start.2 = (bf16[512,64]{1,0:T(8,128)(2,1)}, bf16[512,64]{1,0:T(8,128)(2,1)S(1)}, u32[]{:S(2)}) copy-start(bf16[512,64]{1,0:T(8,128)(2,1)S(1)} %rev.41) | copy-start | bytes 196612
  71.6 11.9 %copy-start.44 = (f32[6]{0:T(128)S(1)}, f32[6]{0:T(128)}, u32[]{:S(2)}) copy-start(f32[6]{0:T(128)} %get-tuple-element.215) | copy-start | bytes 76
  71.7 16.0 %copy-start.23 = (f32[512,6]{0,1:T(8,128)S(1)}, f32[512,6]{0,1:T(8,128)}, u32[]{:S(2)}) copy-start(f32[512,6]{0,1:T(8,128)} %rev.34) | copy-start | bytes 36868
  71.7 16.0 %copy-start.42 = (f32[6]{0:T(128)S(1)}, f32[6]{0:T(128)}, u32[]{:S(2)}) copy-start(f32[6]{0:T(128)} %get-tuple-element.208) | copy-start | bytes 76
  71.7 16.0 %copy-start.43 = (f32[6]{0:T(128)S(1)}, f32[6]{0:T(128)}, u32[]{:S(2)}) copy-start(f32[6]{0:T(128)} %get-tuple-element.214) | copy-start | bytes 76
  86.7 6.0 %copy-start.36 = (f32[6]{0:T(128)}, f32[6]{0:T(128)S(1)}, u32[]{:S(2)}) copy-start(f32[6]{0:T(128)S(1)} %slice_reduce_fusion.1) | copy-start | bytes 76
  87.7 5.0 %copy-start.26 = (f32[512,6]{0,1:T(8,128)}, f32[512,6]{0,1:T(8,128)S(1)}, u32[]{:S(2)}) copy-start(f32[512,6]{0,1:T(8,128)S(1)} %rev.39) | copy-start | bytes 36868
  93.9 8.6 %copy-start.35 = (f32[6]{0:T(128)S(1)}, f32[6]{0:T(128)}, u32[]{:S(2)}) copy-start(f32[6]{0:T(128)} %copy-done.34) | copy-start | bytes 76
  95.2 4.2 %copy-start.31 = (f32[1,6,512]{2,1,0:T(8,128)S(1)}, f32[1,6,512]{2,1,0:T(8,128)}, u32[]{:S(2)}) copy-start(f32[1,6,512]{2,1,0:T(8,128)} %get-tuple-element.231) | copy-start | bytes 36868
  95.2 25.9 %copy-start.37 = (f32[6]{0:T(128)S(1)}, f32[6]{0:T(128)}, u32[]{:S(2)}) copy-start(f32[6]{0:T(128)} %copy-done.36) | copy-start | bytes 76
  95.2 25.9 %copy-start.39 = (f32[6]{0:T(128)S(1)}, f32[6]{0:T(128)}, u32[]{:S(2)}) copy-start(f32[6]{0:T(128)} %copy-done.38) | copy-start | bytes 76
  95.2 43.1 %copy-start.24 = (f32[512,6]{0,1:T(8,128)S(1)}, f32[512,6]{0,1:T(8,128)}, u32[]{:S(2)}) copy-start(f32[512,6]{0,1:T(8,128)} %rev.34) | copy-start | bytes 36868
  95.3 43.2 %copy-start.9 = (bf16[512,384]{0,1:T(8,128)(2,1)S(1)}, bf16[512,384]{0,1:T(8,128)(2,1)}, u32[]{:S(2)}) copy-start(bf16[512,384]{0,1:T(8,128)(2,1)} %copy.110) | copy-start | bytes 1179652
  95.3 43.2 %copy-start.15 = (bf16[512,64]{0,1:T(8,128)(2,1)S(1)}, bf16[512,64]{0,1:T(8,128)(2,1)}, u32[]{:S(2)}) copy-start(bf16[512,64]{0,1:T(8,128)(2,1)} %copy-done.14) | copy-start | bytes 196612
  95.3 44.3 %copy-start.18 = (f32[1,6,512]{2,1,0:T(8,128)S(1)}, f32[1,6,512]{2,1,0:T(8,128)}, u32[]{:S(2)}) copy-start(f32[1,6,512]{2,1,0:T(8,128)} %copy-done.17) | copy-start | bytes 36868
  95.3 44.9 %copy-start.13 = (f32[1,6,4,128]{3,2,1,0:T(4,128)S(1)}, f32[1,6,4,128]{3,2,1,0:T(4,128)}, u32[]{:S(2)}) copy-start(f32[1,6,4,128]{3,2,1,0:T(4,128)} %copy-done.12) | copy-start | bytes 36868
  95.3 44.9 %copy-start.20 = (f32[1,6,512]{2,1,0:T(8,128)S(1)}, f32[1,6,512]{2,1,0:T(8,128)}, u32[]{:S(2)}) copy-start(f32[1,6,512]{2,1,0:T(8,128)} %copy-done.19) | copy-start | bytes 36868
  95.8 45.0 %copy-start.48 = (pred[8]{0:T(512)(128)(4,1)S(1)}, pred[8]{0:T(512)(128)(4,1)}, u32[]{:S(2)}) copy-start(pred[8]{0:T(512)(128)(4,1)} %get-tuple-element.232) | copy-start | bytes 28
  95.8 45.7 %copy-start.47 = (pred[8]{0:T(512)(128)(4,1)S(1)}, pred[8]{0:T(512)(128)(4,1)}, u32[]{:S(2)}) copy-start(pred[8]{0:T(512)(128)(4,1)} %get-tuple-element.233) | copy-start | bytes 28
  96.0 42.7 %copy-start.21 = (f32[1,6,64,64]{3,2,1,0:T(8,128)S(1)}, f32[1,6,64,64]{3,2,1,0:T(8,128)}, u32[]{:S(2)}) copy-start(f32[1,6,64,64]{3,2,1,0:T(8,128)} %fusion.39) | copy-start | bytes 294916
  99.3 129.3 %all-gather.9.cloned.1.call-start = ((), (), s32[]{:S(2)}) async-start(), calls=%async_computation.3 | async-start | bytes 3538944 | tf_op jit(solution)/shard_map/all_gather | solution.py:102
  142.1 4.4 %copy-start.3 = (f32[512,512]{1,0:T(8,128)S(1)}, f32[512,512]{1,0:T(8,128)}, u32[]{:S(2)}) copy-start(f32[512,512]{1,0:T(8,128)} %fusion.144) | copy-start | bytes 3145732
  142.1 4.4 %copy-start.16 = (pred[512,512]{1,0:T(8,128)(4,1)S(1)}, pred[512,512]{1,0:T(8,128)(4,1)}, u32[]{:S(2)}) copy-start(pred[512,512]{1,0:T(8,128)(4,1)} %iota_compare_fusion.2) | copy-start | bytes 786436
  142.1 4.4 %copy-start.27 = (f32[512,6]{0,1:T(8,128)S(1)}, f32[512,6]{0,1:T(8,128)}, u32[]{:S(2)}) copy-start(f32[512,6]{0,1:T(8,128)} %copy-done.26) | copy-start | bytes 36868
  142.1 4.4 %copy-start.32 = (f32[6,512]{1,0:T(8,128)S(1)}, f32[6,512]{1,0:T(8,128)}, u32[]{:S(2)}) copy-start(f32[6,512]{1,0:T(8,128)} %fusion.124) | copy-start | bytes 36868
  142.2 4.4 %copy-start.51 = (f32[6]{0:T(128)S(1)}, f32[6]{0:T(128)}, u32[]{:S(2)}) copy-start(f32[6]{0:T(128)} %get-tuple-element.191) | copy-start | bytes 76
  146.5 3.0 %copy-start.4 = (f32[512,512]{1,0:T(8,128)S(1)}, f32[512,512]{1,0:T(8,128)}, u32[]{:S(2)}) copy-start(f32[512,512]{1,0:T(8,128)} %fusion.143) | copy-start | bytes 3145732
  146.6 3.0 %copy-start.10 = (bf16[512,384]{0,1:T(8,128)(2,1)S(1)}, bf16[512,384]{0,1:T(8,128)(2,1)}, u32[]{:S(2)}) copy-start(bf16[512,384]{0,1:T(8,128)(2,1)} %copy.110) | copy-start | bytes 1179652
  152.6 9.0 %copy-start.29 = (f32[512,6]{0,1:T(8,128)S(1)}, f32[512,6]{0,1:T(8,128)}, u32[]{:S(2)}) copy-start(f32[512,6]{0,1:T(8,128)} %get-tuple-element.150) | copy-start | bytes 36868
  152.6 9.0 %copy-start.46 = (f32[6]{0:T(128)S(1)}, f32[6]{0:T(128)}, u32[]{:S(2)}) copy-start(f32[6]{0:T(128)} %get-tuple-element.228) | copy-start | bytes 76
  159.2 4.0 %copy-start.30 = (f32[512,6]{0,1:T(8,128)S(1)}, f32[512,6]{0,1:T(8,128)}, u32[]{:S(2)}) copy-start(f32[512,6]{0,1:T(8,128)} %get-tuple-element.148) | copy-start | bytes 36868
  159.2 4.0 %copy-start.45 = (f32[6]{0:T(128)S(1)}, f32[6]{0:T(128)}, u32[]{:S(2)}) copy-start(f32[6]{0:T(128)} %get-tuple-element.224) | copy-start | bytes 76
  165.2 65.7 %copy-start.28 = (f32[512,6]{0,1:T(8,128)S(1)}, f32[512,6]{0,1:T(8,128)}, u32[]{:S(2)}) copy-start(f32[512,6]{0,1:T(8,128)} %get-tuple-element.159) | copy-start | bytes 36868
  167.3 63.7 %copy-start.5 = (f32[512,6,64]{0,2,1:T(8,128)S(1)}, f32[512,6,64]{0,2,1:T(8,128)}, u32[]{:S(2)}) copy-start(f32[512,6,64]{0,2,1:T(8,128)} %fusion.28) | copy-start | bytes 2359300
  167.3 67.9 %all-to-all-start.2 = ((bf16[8,64,384]{2,1,0:T(8,128)(2,1)}), bf16[8,64,384]{2,1,0:T(8,128)(2,1)}, u32[]{:S(2)}, u32[]{:S(2)}) async-start(bf16[8,64,384]{2,1,0:T(8,128)(2,1)} %copy.137), calls=%async_computation.2 | async-start | bytes 786432 | tf_op jit(solution)/shard_map/all_to_all | solution.py:218
  228.6 4.4 %copy-start.8 = (bf16[512,64]{0,1:T(8,128)(2,1)S(1)}, bf16[512,64]{0,1:T(8,128)(2,1)}, u32[]{:S(2)}) copy-start(bf16[512,64]{0,1:T(8,128)(2,1)} %copy-done.7) | copy-start | bytes 196612
  (11 other events, 25.0 us)
Sparse Core Ops, SparseCore 0:
  99.5 59.6 all-gather.10
  161.4 67.2 all-gather.8
where the time goes:
time: 246 us; the launch traced here: 245 us
  waiting for transfers between devices  80.4 us (33%)
  other arithmetic  36.7 us (15%)
  blocking collectives  35.1 us (14%)
  matrix products  32.2 us (13%)
  starting transfers between devices  23 us (9%)
  local copies, waits for them, and re-layouts  22.9 us (9%)
  between operations  14.3 us (6%)
    all_gather x2, waiting for transfers between devices, carries(): lax.all_gather(total_states, 'seq', axis=0, tiled=True)  63.7 us
    all_gather x2, blocking collectives, carries(): lax.all_gather(total_logs, 'seq', axis=0, tiled=True)  35.1 us
    dot_general x4, matrix products, one_block(): jnp.einsum('hts,shp->thp', mixing, value_part, preferred_element_type=jnp...  14.7 us
    ppermute x1, waiting for transfers between devices, with_halo(): lax.ppermute(lax.slice_in_dim(block, block.shape[dim] - width, None, axis...  8.58 us
    another operation x11, other arithmetic  8.23 us
    all_to_all x1, waiting for transfers between devices, body(): lax.all_to_all(activated, 'seq', split_axis=1, concat_axis=0, tiled=True)  7.43 us
    all_to_all x1, starting transfers between devices, body(): lax.all_to_all(activated, 'seq', split_axis=1, concat_axis=0, tiled=True)  5.99 us
    all_to_all x1, starting transfers between devices, body(): lax.all_to_all(coupling_send, 'seq', split_axis=1, concat_axis=0, tiled=T...  5.79 us
  transfers between devices with their start and end apart: 7, of which 5 were waited for; matrix products, arithmetic and copies ran while one was open for 23% of the time, Pallas kernels for 0%

commit v1 on v0

v1 whole, which is shorter than its diff:
```python
import functools
import jax
import jax.numpy as jnp
from jax import lax
from jax.experimental import pallas as pl
from jax.experimental.pallas import tpu as pltpu
from jax.sharding import PartitionSpec as P

EPSILON = 1e-05
BF = jnp.bfloat16
F32 = jnp.float32
TILE = 128


def mm(a, b):
    return jnp.dot(a, b, preferred_element_type=F32)


def mm_nt(a, b):
    return lax.dot_general(a, b, (((1,), (1,)), ((), ())), preferred_element_type=F32)


def mm_tn(a, b):
    return lax.dot_general(a, b, (((0,), (0,)), ((), ())), preferred_element_type=F32)


def split3(v):
    hi = v.astype(BF)
    rest = v - hi.astype(F32)
    mid = rest.astype(BF)
    lo = (rest - mid.astype(F32)).astype(BF)
    return hi, mid, lo


def iota(shape, dim):
    return lax.broadcasted_iota(jnp.int32, shape, dim)


def kernel(
    n,
    heads,
    state,
    region_ref,
    norm_gain_ref,
    in_w_ref,
    conv_w_ref,
    conv_b_ref,
    coup_w_ref,
    step_w_ref,
    step_b_ref,
    decay_ref,
    skip_ref,
    out_gain_ref,
    out_w_ref,
    out_ref,
    halo,
    pre,
    gate,
    act,
    colbuf,
    xcol,
    xe,
    xo,
    coup,
    cum,
    cum_t,
    step_t,
    own_row,
    own_col,
    msg,
    got,
    ent_out,
    ent_in,
    col_out,
    col_in,
    halo_send,
    halo_recv,
    a_send,
    a_recv,
    s_send,
    s_recv,
    e_send,
    e_recv,
    c_send,
    c_recv,
):
    me = lax.axis_index("seq")
    tokens, width = region_ref.shape[1], region_ref.shape[2]
    inner = out_w_ref.shape[0]
    band = tokens // n
    head = inner // heads
    part = state // n
    head_bits = head.bit_length() - 1
    n_bits = n.bit_length() - 1
    band_bits = band.bit_length() - 1
    groups = 4 * heads

    def peer_of(k):
        return lax.rem(me + k, n)

    def source_of(k):
        return lax.rem(me + n - k, n)

    barrier = pltpu.get_barrier_semaphore()

    def greet(k, _):
        pl.semaphore_signal(barrier, inc=1, device_id={"seq": peer_of(k)})
        return 0

    lax.fori_loop(1, n, greet, 0)
    pl.semaphore_wait(barrier, n - 1)

    def halo_copy(slot, device):
        return pltpu.make_async_remote_copy(
            src_ref=region_ref.at[0],
            dst_ref=halo.at[slot],
            send_sem=halo_send.at[slot],
            recv_sem=halo_recv.at[slot],
            device_id={"seq": device},
        )

    @pl.when(me < n - 1)
    def _():
        halo_copy(0, me + 1).start()

    @pl.when(me > 0)
    def _():
        halo_copy(1, me - 1).start()

    def normed(values):
        mean_square = jnp.mean(values * values, axis=-1, keepdims=True)
        return (values * lax.rsqrt(mean_square + EPSILON) * norm_gain_ref[...]).astype(BF)

    edge = jnp.zeros((8, inner), F32)
    for a in range(3):
        pre[a, 0:8, :] = edge
        pre[a, tokens + 8 : tokens + 16, :] = edge
    own = mm(normed(region_ref[0].astype(F32)), in_w_ref[...]).astype(BF)
    pre[1, 8 : tokens + 8, :] = own[:, :inner].astype(F32)
    gate[...] = own[:, inner:]

    @pl.when(me < n - 1)
    def _():
        halo_copy(1, me + 1).wait_recv()
        halo_copy(0, me + 1).wait_send()

    @pl.when(me == n - 1)
    def _():
        halo[1] = jnp.zeros((tokens, width), BF)

    @pl.when(me > 0)
    def _():
        halo_copy(0, me - 1).wait_recv()
        halo_copy(1, me - 1).wait_send()

    @pl.when(me == 0)
    def _():
        halo[0] = jnp.zeros((tokens, width), BF)

    for slot, a in ((0, 0), (1, 2)):
        rim = mm(normed(halo[slot].astype(F32)), in_w_ref[:, :inner]).astype(BF)
        pre[a, 8 : tokens + 8, :] = rim.astype(F32)

    per = TILE // band if band < TILE else 1
    for c in range(tokens // TILE):
        summed = conv_b_ref[...]
        for a in range(3):
            for b in range(3):
                first = c * TILE + 7 + b
                tap = 3 * a + b
                summed = summed + pre[a, first : first + TILE, :] * conv_w_ref[tap : tap + 1, :]
        done = (summed / (1.0 + jnp.exp(-summed))).astype(BF)
        if band <= TILE:
            act[c * per : (c + 1) * per] = done.reshape(per, band, inner)
        else:
            where = c * TILE // band
            start = c * TILE % band
            act[where, start : start + TILE] = done

    def a_copy(k, chunk, place):
        return pltpu.make_async_remote_copy(
            src_ref=act.at[chunk],
            dst_ref=colbuf.at[place],
            send_sem=a_send.at[k],
            recv_sem=a_recv.at[k],
            device_id={"seq": chunk},
        )

    def s_copy(p, k, chunk, place):
        return pltpu.make_async_remote_copy(
            src_ref=msg.at[p, chunk],
            dst_ref=got.at[p, place],
            send_sem=s_send.at[p, k],
            recv_sem=s_recv.at[p, k],
            device_id={"seq": chunk},
        )

    def e_copy(p, k, chunk, place):
        return pltpu.make_async_remote_copy(
            src_ref=ent_out.at[p, chunk],
            dst_ref=ent_in.at[p, place],
            send_sem=e_send.at[p, k],
            recv_sem=e_recv.at[p, k],
            device_id={"seq": chunk},
        )

    def c_copy(k, chunk, place):
        return pltpu.make_async_remote_copy(
            src_ref=col_out.at[chunk],
            dst_ref=col_in.at[place],
            send_sem=c_send.at[k],
            recv_sem=c_recv.at[k],
            device_id={"seq": chunk},
        )

    def start_all(make):
        def one(k, _):
            make(k, peer_of(k), me).start()
            return 0

        lax.fori_loop(1, n, one, 0)

    def wait_all(make):
        def one(k, _):
            make(k, peer_of(k), source_of(k)).wait_recv()
            return 0

        lax.fori_loop(1, n, one, 0)

    def wait_sent(make):
        def one(k, _):
            make(k, peer_of(k), source_of(k)).wait_send()
            return 0

        lax.fori_loop(1, n, one, 0)

    start_all(a_copy)
    colbuf[pl.ds(me, 1)] = act[pl.ds(me, 1)]

    group_lane = iota((1, groups), 1)
    behind_lane = lax.rem(group_lane, 2 * heads) >= heads
    lower = (iota((tokens, tokens), 0) >= iota((tokens, tokens), 1)).astype(BF)
    eye = (iota((groups, groups), 0) == iota((groups, groups), 1)).astype(BF)
    spread_row = iota((groups, inner), 0)
    spread_head = jnp.right_shift(iota((groups, inner), 1), head_bits)
    rates = -jnp.exp(decay_ref[...])

    def spreader(base):
        return (spread_row == base + spread_head).astype(BF)

    def expand(v, e):
        hi, mid, lo = split3(v)
        return mm(hi, e) + mm(mid, e) + mm(lo, e)

    def flip_axes(v):
        hi, mid, lo = split3(v)
        return mm_nt(eye, hi) + mm_nt(eye, mid) + mm_nt(eye, lo)

    def prepare(p, x):
        first = p * 4 * state
        coup[p] = mm(x, coup_w_ref[:, first : first + 4 * state]).astype(BF)
        logits = mm(x, step_w_ref[...]) + step_b_ref[...]
        steps = jnp.maximum(logits, 0.0) + jnp.log1p(jnp.exp(-jnp.abs(logits)))
        logs = rates * steps
        hi, mid, lo = split3(logs)
        ahead = mm(lower, hi) + mm(lower, mid) + mm(lower, lo)
        total = ahead[tokens - 1 : tokens, :]
        c = jnp.where(behind_lane, total - ahead + logs, ahead)
        cum[p] = c
        cum_t[p] = flip_axes(c)
        step_t[p] = flip_axes(steps)
        tail = jnp.exp(total - c) * steps
        base = p * 2 * heads
        xf = x.astype(F32)
        spread_a, spread_b = spreader(base), spreader(base + heads)
        totals = jnp.broadcast_to(total, (8, groups))
        for o, e in ((0, spread_a), (1, spread_b)):
            weighted = (xf * expand(tail, e)).astype(BF)
            writer = coup[p, :, 2 * o * state : (2 * o + 1) * state]
            contrib = mm_tn(writer, weighted)
            decay = expand(totals, e)[0:1]
            for d in range(n):
                msg[p, d, o * part : (o + 1) * part, :] = contrib[d * part : (d + 1) * part]
                msg[p, d, 2 * part + o : 2 * part + o + 1, :] = decay
        start_all(functools.partial(s_copy, p))
        got[p, pl.ds(me, 1)] = msg[p, pl.ds(me, 1)]
        def diagonal(o):
            w = coup[p, :, 2 * o * state : (2 * o + 1) * state].astype(F32)
            r = coup[p, :, (2 * o + 1) * state : (2 * o + 2) * state].astype(F32)
            return jnp.sum(w * r, axis=-1, keepdims=True)

        diag = (jnp.where(behind_lane, diagonal(1), diagonal(0)) * steps).astype(BF).astype(F32)
        target = own_col if p else own_row
        target[...] = xf * expand(diag + skip_ref[...], spread_a + spread_b)
        even = jnp.bitwise_and(iota((1, inner), 1), head) == 0
        xe[...] = jnp.where(even, xf, 0.0).astype(BF)
        xo[...] = jnp.where(even, 0.0, xf).astype(BF)

    def mix(p):
        target = own_col if p else own_row

        def tile(i, _):
            t0 = pl.multiple_of(i * TILE, TILE)
            rows = pl.ds(t0, TILE)
            both = coup[p, rows, :]
            ahead = mm_nt(both[:, state : 2 * state], coup[p, :, 0:state])
            behind = mm_nt(both[:, 3 * state : 4 * state], coup[p, :, 2 * state : 3 * state])
            t = iota((TILE, tokens), 0) + t0
            s = iota((TILE, tokens), 1)
            after = t > s
            scores = jnp.where(after, ahead, jnp.where(t < s, behind, 0.0))
            c = cum[p, rows, :]

            def weights(h):
                f = p * 2 * heads + h
                g = f + heads
                lead = c[:, f : f + 1] - cum_t[p, f : f + 1, :]
                back = c[:, g : g + 1] - cum_t[p, g : g + 1, :]
                step = jnp.where(after, step_t[p, f : f + 1, :], step_t[p, g : g + 1, :])
                return (scores * jnp.exp(jnp.minimum(lead, back)) * step).astype(BF)

            for j in range(heads // 2):
                lanes = slice(2 * j * head, 2 * (j + 1) * head)
                inside = mm(weights(2 * j), xe[:, lanes]) + mm(weights(2 * j + 1), xo[:, lanes])
                target[rows, lanes] += inside
            return 0

        lax.fori_loop(0, tokens // TILE, tile, 0)

    def scan(p):
        wait_all(functools.partial(s_copy, p))
        entry = jnp.zeros((part, inner), F32)
        ahead = []
        for i in range(n):
            ahead.append(entry)
            decay = jnp.exp(got[p, i, 2 * part : 2 * part + 1, :])
            entry = decay * entry + got[p, i, 0:part, :]
        entry = jnp.zeros((part, inner), F32)
        for i in reversed(range(n)):
            pieces = [ahead[i], entry]
            if 2 * part < 16:
                pieces.append(jnp.zeros((16 - 2 * part, inner), F32))
            ent_out[p, i] = jnp.concatenate(pieces, axis=0).astype(BF)
            decay = jnp.exp(got[p, i, 2 * part + 1 : 2 * part + 2, :])
            entry = decay * entry + got[p, i, part : 2 * part, :]
        start_all(functools.partial(e_copy, p))
        ent_in[p, pl.ds(me, 1)] = ent_out[p, pl.ds(me, 1)]

    def finish(p):
        wait_all(functools.partial(e_copy, p))
        target = own_col if p else own_row
        arrived = [ent_in[p, i].astype(F32) for i in range(n)]
        grown = jnp.exp(cum[p])
        base = p * 2 * heads
        result = target[...]
        for o in range(2):
            entry = jnp.concatenate(
                [v[o * part : (o + 1) * part] for v in arrived], axis=0
            ).astype(BF)
            reader = coup[p, :, (2 * o + 1) * state : (2 * o + 2) * state]
            result = result + mm(reader, entry) * expand(grown, spreader(base + o * heads))
        return result

    x_row = act[...].reshape(tokens, inner)
    prepare(0, x_row)
    mix(0)
    wait_all(a_copy)
    place = iota((tokens, tokens), 0)
    cell = iota((tokens, tokens), 1)
    turn = cell == jnp.left_shift(jnp.bitwise_and(place, n - 1), band_bits) + jnp.right_shift(place, n_bits)
    xcol[...] = mm(turn.astype(BF), colbuf[...].reshape(tokens, inner)).astype(BF)
    prepare(1, xcol[...])
    scan(0)
    mix(1)
    scan(1)
    column = finish(1).astype(BF)
    back = cell == jnp.left_shift(jnp.bitwise_and(place, band - 1), n_bits) + jnp.right_shift(place, band_bits)
    col_out[...] = mm(back.astype(BF), column).astype(BF).reshape(n, band, inner)
    start_all(c_copy)
    col_in[pl.ds(me, 1)] = col_out[pl.ds(me, 1)]
    row_total = finish(0)
    g = gate[...].astype(F32)
    own_row[...] = row_total
    own_col[...] = g / (1.0 + jnp.exp(-g))
    wait_all(c_copy)
    for c in range(tokens // TILE):
        rows = slice(c * TILE, (c + 1) * TILE)
        if band <= TILE:
            col = col_in[c * per : (c + 1) * per].reshape(TILE, inner)
        else:
            start = c * TILE % band
            col = col_in[c * TILE // band, start : start + TILE]
        gated = (own_row[rows, :] + col.astype(F32)) * own_col[rows, :]
        mean_square = jnp.mean(gated * gated, axis=-1, keepdims=True)
        normy = (gated * lax.rsqrt(mean_square + EPSILON) * out_gain_ref[...]).astype(BF)
        out_ref[0, rows, :] = (
            region_ref[0, rows, :].astype(F32) + mm(normy, out_w_ref[...])
        ).astype(BF)
    wait_sent(a_copy)
    for p in range(2):
        wait_sent(functools.partial(s_copy, p))
        wait_sent(functools.partial(e_copy, p))
    wait_sent(c_copy)


def body(n, *args):
    region = args[0]
    rows, tokens, width = region.shape
    inner = args[11].shape[0]
    groups = args[7].shape[0]
    heads = groups // 4
    state = args[5].shape[1] // 8
    band = tokens // n
    part = state // n
    flat = [v if v.ndim > 1 else v.reshape(1, -1) for v in args]
    msg_rows = 2 * part + 2
    ent_rows = max(16, 2 * part)
    dma = pltpu.SemaphoreType.DMA
    vmem = pltpu.VMEM
    return pl.pallas_call(
        functools.partial(kernel, n, heads, state),
        out_shape=jax.ShapeDtypeStruct(region.shape, BF),
        in_specs=[pl.BlockSpec(memory_space=pltpu.VMEM)] * len(flat),
        out_specs=pl.BlockSpec(memory_space=pltpu.VMEM),
        scratch_shapes=[
            vmem((2, tokens, width), BF),
            vmem((3, tokens + 16, inner), F32),
            vmem((tokens, inner), BF),
            vmem((n, band, inner), BF),
            vmem((n, band, inner), BF),
            vmem((tokens, inner), BF),
            vmem((tokens, inner), BF),
            vmem((tokens, inner), BF),
            vmem((2, tokens, 4 * state), BF),
            vmem((2, tokens, groups), F32),
            vmem((2, groups, tokens), F32),
            vmem((2, groups, tokens), F32),
            vmem((tokens, inner), F32),
            vmem((tokens, inner), F32),
            vmem((2, n, msg_rows, inner), F32),
            vmem((2, n, msg_rows, inner), F32),
            vmem((2, n, ent_rows, inner), BF),
            vmem((2, n, ent_rows, inner), BF),
            vmem((n, band, inner), BF),
            vmem((n, band, inner), BF),
            dma((2,)),
            dma((2,)),
            dma((n,)),
            dma((n,)),
            dma((2, n)),
            dma((2, n)),
            dma((2, n)),
            dma((2, n)),
            dma((n,)),
            dma((n,)),
        ],
        compiler_params=pltpu.CompilerParams(
            collective_id=0, has_side_effects=True, vmem_limit_bytes=50 * 1024 * 1024
        ),
    )(*flat)


def solution(mesh):
    in_specs = (P(("dp", "seq"), None, None),) + (P(),) * 11
    return jax.shard_map(
        functools.partial(body, mesh.shape["seq"]),
        mesh=mesh,
        in_specs=in_specs,
        out_specs=P(("dp", "seq"), None, None),
        check_vma=False,
    )
```

time: 246 us -> 65 us (0.26)
  waiting for transfers between devices: 80.4 us -> 0 us
  Pallas kernels: 0 us -> 59.6 us
  other arithmetic: 36.7 us -> 0 us
  blocking collectives: 35.1 us -> 0 us
  matrix products: 32.2 us -> 0 us
  starting transfers between devices: 23 us -> 0 us
  local copies, waits for them, and re-layouts: 22.9 us -> 5.06 us
  between operations: 14.3 us -> 0.11 us
    all_gather x2 -> x0, waiting for transfers between devices: 63.7 us -> none  [carries(): lax.all_gather(total_states, 'seq', axis=0, tiled=True)]
    pallas_call x0 -> x1, Pallas kernels: none -> 59.6 us  [body(): pl.pallas_call(functools.partial(kernel, n, heads, state), out_shape=jax....]
    all_gather x2 -> x0, blocking collectives: 35.1 us -> none  [carries(): lax.all_gather(total_logs, 'seq', axis=0, tiled=True)]
    dot_general x21 -> x0, matrix products: 32.2 us -> none  [the longest x4 14.7 us: one_block(): jnp.einsum('hts,shp->thp', mixing, value_part, preferred_element_type=jnp...]
    all_to_all x3 -> x0, starting transfers between devices: 16 us -> none  [the longest x1 5.99 us: body(): lax.all_to_all(activated, 'seq', split_axis=1, concat_axis=0, tiled=True)]
    another operation x15 -> x0, other arithmetic: 9.84 us -> none
    ppermute x2 -> x0, waiting for transfers between devices: 9.22 us -> none  [the longest x1 8.58 us: with_halo(): lax.ppermute(lax.slice_in_dim(block, block.shape[dim] - width, None, axis...]
    all_to_all x3 -> x0, waiting for transfers between devices: 7.43 us -> none  [the longest x1 7.43 us: body(): lax.all_to_all(activated, 'seq', split_axis=1, concat_axis=0, tiled=True)]
  transfers between devices with their start and end apart: 7 -> 0, of which waited for: 5 -> 0; matrix products, arithmetic and copies ran while one was open for 23% -> 0% of each run, Pallas kernels for 0% -> 0%
where the time goes in v1:
time: 65 us; the launch traced here: 64.8 us
  Pallas kernels  59.6 us (92%)
  local copies, waits for them, and re-layouts  5.06 us (8%)
    pallas_call x1, Pallas kernels, body(): pl.pallas_call(functools.partial(kernel, n, heads, state), out_shape=jax....  59.6 us
    unnamed x23, local copies, waits for them, and re-layouts  4.25 us

profile of v1, /device:TPU:0, one launch (start us, length us, event | category | flops | bytes accessed | tf_op | source)
XLA Modules:
  0.0 64.8 jit_solution(17230718987560976750)
XLA Ops:
  0.0 0.0 copy-start.8
  0.0 0.7 %copy-done.8 = f32[384]{0:T(512)S(1)} copy-done((f32[384]{0:T(512)S(1)}, f32[384]{0:T(512)}, u32[]{:S(2)}) %copy-start.8) | copy-done | bytes 1560
  0.7 0.0 copy-start.9
  0.7 0.7 %copy-done.9 = f32[384]{0:T(512)S(1)} copy-done((f32[384]{0:T(512)S(1)}, f32[384]{0:T(512)}, u32[]{:S(2)}) %copy-start.9) | copy-done | bytes 1560
  1.4 0.0 copy-start.7
  1.4 0.9 %copy.14.step_w_ref = bf16[384,24]{1,0:T(8,128)(2,1)S(1)} copy(bf16[384,24]{0,1:T(8,128)(2,1)} %param.18) | data formatting | bytes 36864 | tf_op args[6]
  2.3 0.0 copy-start
  2.3 1.1 %copy.15.out_w_ref = bf16[384,192]{1,0:T(8,128)(2,1)S(1)} copy(bf16[384,192]{0,1:T(8,128)(2,1)} %param.23) | data formatting | bytes 294912 | tf_op args[11]
  3.4 0.0 copy-done.7
  3.4 0.0 copy-start.1
  3.4 0.0 copy-start.2
  3.4 0.0 copy-start.3
  3.4 0.0 copy-start.4
  3.4 0.0 copy-start.5
  3.4 0.0 copy-start.6
  3.4 0.1 copy.13.region_ref
  3.6 0.0 copy-done
  3.6 0.7 %copy-done.1 = bf16[192,768]{1,0:T(8,128)(2,1)S(1)} copy-done((bf16[192,768]{1,0:T(8,128)(2,1)S(1)}, bf16[192,768]{1,0:T(8,128)(2,1)}, u32[]{:S(2)}) %copy-start.1) | copy-done | bytes 294936
  4.3 0.0 copy-done.2
  4.3 0.0 copy-done.3
  4.3 0.0 copy-done.4
  4.3 0.0 copy-done.5
  4.4 0.0 copy-done.6
  4.4 59.6 %shard_map.118 = bf16[1,512,192]{2,1,0:T(8,128)(2,1)S(1)} custom-call(bf16[1,512,192]{2,1,0:T(8,128)(2,1)S(1)} %copy.13.region_ref, f32[1,192]{1,0:T(1,128)S(1)} %bitcast.4, bf16[192,768]{1,0:T(8,128)(2,1)S(1)} %copy-done.1, f32[9,384]{1,0:T(8,128)S(1)} %copy-done.2, f32[1,384]{1,0:T(1,128)S(1)} %reshape.19.conv_b_ref, bf16[384,512]{1,0:T(8,128)(2,1)S(1)} %copy-done, ...), custom_call_target="tpu_custom_call" | custom-call | tf_op jit(solution)/shard_map/pallas_call | solution.py:420
  64.0 0.8 %copy.16 = bf16[1,512,192]{1,2,0:T(8,128)(2,1)} copy(bf16[1,512,192]{2,1,0:T(8,128)(2,1)S(1)} %shard_map.118) | data formatting | bytes 393216 | tf_op jit(solution)/shard_map/pallas_call | solution.py:420
  (2 shorter events, 0.0 us)
Async XLA Ops:
  0.0 0.7 %copy-start.8 = (f32[384]{0:T(512)S(1)}, f32[384]{0:T(512)}, u32[]{:S(2)}) copy-start(f32[384]{0:T(512)} %param.16) | copy-start | bytes 4612
  0.7 0.7 %copy-start.9 = (f32[384]{0:T(512)S(1)}, f32[384]{0:T(512)}, u32[]{:S(2)}) copy-start(f32[384]{0:T(512)} %param.22) | copy-start | bytes 4612
  1.4 2.0 %copy-start.7 = (bf16[1,512,192]{1,2,0:T(8,128)(2,1)S(1)}, bf16[1,512,192]{1,2,0:T(8,128)(2,1)}, u32[]{:S(2)}) copy-start(bf16[1,512,192]{1,2,0:T(8,128)(2,1)} %param.12) | copy-start | bytes 589828
  2.3 1.3 %copy-start = (bf16[384,512]{1,0:T(8,128)(2,1)S(1)}, bf16[384,512]{1,0:T(8,128)(2,1)}, u32[]{:S(2)}) copy-start(bf16[384,512]{1,0:T(8,128)(2,1)} %coup_w_ref.1) | copy-start | bytes 1179652
  3.4 1.0 %copy-start.1 = (bf16[192,768]{1,0:T(8,128)(2,1)S(1)}, bf16[192,768]{1,0:T(8,128)(2,1)}, u32[]{:S(2)}) copy-start(bf16[192,768]{1,0:T(8,128)(2,1)} %in_w_ref.1) | copy-start | bytes 884740
  3.4 1.0 %copy-start.2 = (f32[9,384]{1,0:T(8,128)S(1)}, f32[9,384]{1,0:T(8,128)}, u32[]{:S(2)}) copy-start(f32[9,384]{1,0:T(8,128)} %conv_w_ref.1) | copy-start | bytes 41476
  3.4 0.9 %copy-start.3 = (f32[192]{0:T(256)S(1)}, f32[192]{0:T(256)}, u32[]{:S(2)}) copy-start(f32[192]{0:T(256)} %param.13) | copy-start | bytes 2308
  3.4 0.9 %copy-start.4 = (f32[24]{0:T(128)S(1)}, f32[24]{0:T(128)}, u32[]{:S(2)}) copy-start(f32[24]{0:T(128)} %param.19) | copy-start | bytes 292
  3.4 0.9 %copy-start.5 = (f32[24]{0:T(128)S(1)}, f32[24]{0:T(128)}, u32[]{:S(2)}) copy-start(f32[24]{0:T(128)} %param.20) | copy-start | bytes 292
  3.4 0.9 %copy-start.6 = (f32[24]{0:T(128)S(1)}, f32[24]{0:T(128)}, u32[]{:S(2)}) copy-start(f32[24]{0:T(128)} %param.21) | copy-start | bytes 292

commit v2 on v1

--- a/solution.py
+++ b/solution.py
@@ -69,6 +69,8 @@
     own_col,
     msg,
     got,
+    tot,
+    got_tot,
     ent_out,
     ent_in,
     col_out,
@@ -79,6 +81,8 @@
     a_recv,
     s_send,
     s_recv,
+    t_send,
+    t_recv,
     e_send,
     e_recv,
     c_send,
@@ -86,7 +90,7 @@
 ):
     me = lax.axis_index("seq")
     tokens, width = region_ref.shape[1], region_ref.shape[2]
-    inner = out_w_ref.shape[0]
+    inner = out_w_ref.shape[1]
     band = tokens // n
     head = inner // heads
     part = state // n
@@ -195,6 +199,15 @@
             device_id={"seq": chunk},
         )
 
+    def t_copy(p, k, chunk, place):
+        return pltpu.make_async_remote_copy(
+            src_ref=tot.at[p],
+            dst_ref=got_tot.at[p, place],
+            send_sem=t_send.at[p, k],
+            recv_sem=t_recv.at[p, k],
+            device_id={"seq": chunk},
+        )
+
     def e_copy(p, k, chunk, place):
         return pltpu.make_async_remote_copy(
             src_ref=ent_out.at[p, chunk],
@@ -246,11 +259,12 @@
     rates = -jnp.exp(decay_ref[...])
 
     def spreader(base):
-        return (spread_row == base + spread_head).astype(BF)
+        return (spread_row == base + spread_head).astype(F32)
 
     def expand(v, e):
-        hi, mid, lo = split3(v)
-        return mm(hi, e) + mm(mid, e) + mm(lo, e)
+        hi, mid, lo = (piece.astype(F32) for piece in split3(v))
+        pieces = jnp.concatenate([hi, mid, lo], axis=1).astype(BF)
+        return mm(pieces, jnp.concatenate([e, e, e], axis=0).astype(BF))
 
     def flip_axes(v):
         hi, mid, lo = split3(v)
@@ -259,7 +273,7 @@
     def prepare(p, x):
         first = p * 4 * state
         coup[p] = mm(x, coup_w_ref[:, first : first + 4 * state]).astype(BF)
-        logits = mm(x, step_w_ref[...]) + step_b_ref[...]
+        logits = mm_nt(x, step_w_ref[...]) + step_b_ref[...]
         steps = jnp.maximum(logits, 0.0) + jnp.log1p(jnp.exp(-jnp.abs(logits)))
         logs = rates * steps
         hi, mid, lo = split3(logs)
@@ -273,15 +287,19 @@
         base = p * 2 * heads
         xf = x.astype(F32)
         spread_a, spread_b = spreader(base), spreader(base + heads)
-        totals = jnp.broadcast_to(total, (8, groups))
+        tot[p, :, 0:groups] = jnp.broadcast_to(total, (8, groups))
+        start_all(functools.partial(t_copy, p))
+        got_tot[p, pl.ds(me, 1)] = tot[p][None]
+        contribs = []
         for o, e in ((0, spread_a), (1, spread_b)):
             weighted = (xf * expand(tail, e)).astype(BF)
             writer = coup[p, :, 2 * o * state : (2 * o + 1) * state]
-            contrib = mm_tn(writer, weighted)
-            decay = expand(totals, e)[0:1]
-            for d in range(n):
-                msg[p, d, o * part : (o + 1) * part, :] = contrib[d * part : (d + 1) * part]
-                msg[p, d, 2 * part + o : 2 * part + o + 1, :] = decay
+            contribs.append(mm_tn(writer, weighted))
+        for d in range(n):
+            pieces = [v[d * part : (d + 1) * part] for v in contribs]
+            if 2 * part < 16:
+                pieces.append(jnp.zeros((16 - 2 * part, inner), F32))
+            msg[p, d] = jnp.concatenate(pieces, axis=0).astype(BF)
         start_all(functools.partial(s_copy, p))
         got[p, pl.ds(me, 1)] = msg[p, pl.ds(me, 1)]
         def diagonal(o):
@@ -296,7 +314,7 @@
         xe[...] = jnp.where(even, xf, 0.0).astype(BF)
         xo[...] = jnp.where(even, 0.0, xf).astype(BF)
 
-    def mix(p):
+    def mix(p, first, last):
         target = own_col if p else own_row
 
         def tile(i, _):
@@ -325,24 +343,29 @@
                 target[rows, lanes] += inside
             return 0
 
-        lax.fori_loop(0, tokens // TILE, tile, 0)
+        lax.fori_loop(first, last, tile, 0)
 
     def scan(p):
+        wait_all(functools.partial(t_copy, p))
+        base = p * 2 * heads
+        totals = jnp.exp(
+            jnp.concatenate([got_tot[p, i, 0:8, 0:groups] for i in range(n)], axis=0)
+        )
+        fade_a = expand(totals, spreader(base))
+        fade_b = expand(totals, spreader(base + heads))
         wait_all(functools.partial(s_copy, p))
         entry = jnp.zeros((part, inner), F32)
         ahead = []
         for i in range(n):
             ahead.append(entry)
-            decay = jnp.exp(got[p, i, 2 * part : 2 * part + 1, :])
-            entry = decay * entry + got[p, i, 0:part, :]
+            entry = fade_a[8 * i : 8 * i + 1] * entry + got[p, i].astype(F32)[0:part]
         entry = jnp.zeros((part, inner), F32)
         for i in reversed(range(n)):
             pieces = [ahead[i], entry]
             if 2 * part < 16:
                 pieces.append(jnp.zeros((16 - 2 * part, inner), F32))
             ent_out[p, i] = jnp.concatenate(pieces, axis=0).astype(BF)
-            decay = jnp.exp(got[p, i, 2 * part + 1 : 2 * part + 2, :])
-            entry = decay * entry + got[p, i, part : 2 * part, :]
+            entry = fade_b[8 * i : 8 * i + 1] * entry + got[p, i].astype(F32)[part : 2 * part]
         start_all(functools.partial(e_copy, p))
         ent_in[p, pl.ds(me, 1)] = ent_out[p, pl.ds(me, 1)]
 
@@ -363,7 +386,8 @@
 
     x_row = act[...].reshape(tokens, inner)
     prepare(0, x_row)
-    mix(0)
+    tiles = tokens // TILE
+    mix(0, 0, tiles)
     wait_all(a_copy)
     place = iota((tokens, tokens), 0)
     cell = iota((tokens, tokens), 1)
@@ -371,8 +395,9 @@
     xcol[...] = mm(turn.astype(BF), colbuf[...].reshape(tokens, inner)).astype(BF)
     prepare(1, xcol[...])
     scan(0)
-    mix(1)
+    mix(1, 0, tiles // 2)
     scan(1)
+    mix(1, tiles // 2, tiles)
     column = finish(1).astype(BF)
     back = cell == jnp.left_shift(jnp.bitwise_and(place, band - 1), n_bits) + jnp.right_shift(place, band_bits)
     col_out[...] = mm(back.astype(BF), column).astype(BF).reshape(n, band, inner)
@@ -394,11 +419,12 @@
         mean_square = jnp.mean(gated * gated, axis=-1, keepdims=True)
         normy = (gated * lax.rsqrt(mean_square + EPSILON) * out_gain_ref[...]).astype(BF)
         out_ref[0, rows, :] = (
-            region_ref[0, rows, :].astype(F32) + mm(normy, out_w_ref[...])
+            region_ref[0, rows, :].astype(F32) + mm_nt(normy, out_w_ref[...])
         ).astype(BF)
     wait_sent(a_copy)
     for p in range(2):
         wait_sent(functools.partial(s_copy, p))
+        wait_sent(functools.partial(t_copy, p))
         wait_sent(functools.partial(e_copy, p))
     wait_sent(c_copy)
 
@@ -413,7 +439,8 @@
     band = tokens // n
     part = state // n
     flat = [v if v.ndim > 1 else v.reshape(1, -1) for v in args]
-    msg_rows = 2 * part + 2
+    flat[6] = flat[6].T
+    flat[11] = flat[11].T
     ent_rows = max(16, 2 * part)
     dma = pltpu.SemaphoreType.DMA
     vmem = pltpu.VMEM
@@ -437,8 +464,10 @@
             vmem((2, groups, tokens), F32),
             vmem((tokens, inner), F32),
             vmem((tokens, inner), F32),
-            vmem((2, n, msg_rows, inner), F32),
-            vmem((2, n, msg_rows, inner), F32),
+            vmem((2, n, ent_rows, inner), BF),
+            vmem((2, n, ent_rows, inner), BF),
+            vmem((2, 8, 128), F32),
+            vmem((2, n, 8, 128), F32),
             vmem((2, n, ent_rows, inner), BF),
             vmem((2, n, ent_rows, inner), BF),
             vmem((n, band, inner), BF),
@@ -451,6 +480,8 @@
             dma((2, n)),
             dma((2, n)),
             dma((2, n)),
+            dma((2, n)),
+            dma((2, n)),
             dma((n,)),
             dma((n,)),
         ],

time: 65 us -> 58.4 us (0.90)
  Pallas kernels: 59.6 us -> 52.5 us
    pallas_call x1, Pallas kernels: 59.6 us -> 52.5 us  [body(): pl.pallas_call(functools.partial(kernel, n, heads, state), out_shape=jax....]
    reshape x2, local copies, waits for them, and re-layouts: 0.01 us -> 1.42 us  [body(): flat = [v if v.ndim > 1 else v.reshape(1, -1) for v in args]]
    unnamed x23 -> x19, local copies, waits for them, and re-layouts: 4.25 us -> 3.01 us
where the time goes in v2:
time: 58.4 us; the launch traced here: 57.8 us
  Pallas kernels  52.5 us (90%)
  local copies, waits for them, and re-layouts  5.23 us (9%)
    pallas_call x1, Pallas kernels, body(): pl.pallas_call(functools.partial(kernel, n, heads, state), out_shape=jax....  52.5 us
    unnamed x19, local copies, waits for them, and re-layouts  3.01 us
    reshape x2, local copies, waits for them, and re-layouts, body(): flat = [v if v.ndim > 1 else v.reshape(1, -1) for v in args]  1.42 us

profile of v2, /device:TPU:0, one launch (start us, length us, event | category | flops | bytes accessed | tf_op | source)
XLA Modules:
  0.0 57.8 jit_solution(543481630736624212)
XLA Ops:
  0.0 0.0 copy-start
  0.0 0.7 %reshape.19.conv_b_ref = f32[1,384]{1,0:T(1,128)S(1)} reshape(f32[384]{0:T(512)} %param.16) | data formatting | bytes 3072 | tf_op jit(solution)/shard_map/reshape | solution.py:441
  0.7 0.7 %reshape.23.out_gain_ref = f32[1,384]{1,0:T(1,128)S(1)} reshape(f32[384]{0:T(512)} %param.22) | data formatting | bytes 3072 | tf_op jit(solution)/shard_map/reshape | solution.py:441
  1.4 0.0 copy-start.3
  1.4 0.0 copy-start.4
  1.4 0.0 copy-start.5
  1.4 0.0 copy-start.6
  1.4 0.0 copy-start.7
  1.4 0.0 copy-start.8
  1.5 1.1 %copy.13.region_ref = bf16[1,512,192]{2,1,0:T(8,128)(2,1)S(1)} copy(bf16[1,512,192]{1,2,0:T(8,128)(2,1)} %param.12) | data formatting | bytes 393216 | tf_op args[0]
  2.6 0.0 copy-done
  2.6 0.0 copy-done.3
  2.6 0.0 copy-done.4
  2.6 0.0 copy-done.5
  2.6 0.0 copy-done.6
  2.6 0.0 copy-done.7
  2.6 0.0 copy-done.8
  2.6 0.0 copy-start.1
  2.7 1.0 %copy-done.1 = bf16[192,768]{1,0:T(8,128)(2,1)S(1)} copy-done((bf16[192,768]{1,0:T(8,128)(2,1)S(1)}, bf16[192,768]{1,0:T(8,128)(2,1)}, u32[]{:S(2)}) %copy-start.1) | copy-done | bytes 294936
  3.6 0.0 copy-start.2
  3.6 0.9 %copy-done.2 = bf16[384,192]{0,1:T(8,128)(2,1)S(1)} copy-done((bf16[384,192]{0,1:T(8,128)(2,1)S(1)}, bf16[384,192]{0,1:T(8,128)(2,1)}, u32[]{:S(2)}) %copy-start.2) | copy-done | bytes 147480
  4.5 52.5 %shard_map.118 = bf16[1,512,192]{2,1,0:T(8,128)(2,1)S(1)} custom-call(bf16[1,512,192]{2,1,0:T(8,128)(2,1)S(1)} %copy.13.region_ref, f32[1,192]{1,0:T(1,128)S(1)} %bitcast.8, bf16[192,768]{1,0:T(8,128)(2,1)S(1)} %copy-done.1, f32[9,384]{1,0:T(8,128)S(1)} %copy-done.3, f32[1,384]{1,0:T(1,128)S(1)} %reshape.19.conv_b_ref, bf16[384,512]{1,0:T(8,128)(2,1)S(1)} %copy-done, ...), custom_call_target="tpu_custom_call" | custom-call | tf_op jit(solution)/shard_map/pallas_call | solution.py:447
  57.0 0.8 %copy.14 = bf16[1,512,192]{1,2,0:T(8,128)(2,1)} copy(bf16[1,512,192]{2,1,0:T(8,128)(2,1)S(1)} %shard_map.118) | data formatting | bytes 393216 | tf_op jit(solution)/shard_map/pallas_call | solution.py:447
Async XLA Ops:
  0.0 2.6 %copy-start = (bf16[384,512]{1,0:T(8,128)(2,1)S(1)}, bf16[384,512]{1,0:T(8,128)(2,1)}, u32[]{:S(2)}) copy-start(bf16[384,512]{1,0:T(8,128)(2,1)} %coup_w_ref.1) | copy-start | bytes 1179652
  1.4 1.2 %copy-start.3 = (f32[9,384]{1,0:T(8,128)S(1)}, f32[9,384]{1,0:T(8,128)}, u32[]{:S(2)}) copy-start(f32[9,384]{1,0:T(8,128)} %conv_w_ref.1) | copy-start | bytes 41476
  1.4 1.2 %copy-start.4 = (bf16[384,24]{0,1:T(8,128)(2,1)S(1)}, bf16[384,24]{0,1:T(8,128)(2,1)}, u32[]{:S(2)}) copy-start(bf16[384,24]{0,1:T(8,128)(2,1)} %param.18) | copy-start | bytes 55300
  1.4 1.2 %copy-start.5 = (f32[192]{0:T(256)S(1)}, f32[192]{0:T(256)}, u32[]{:S(2)}) copy-start(f32[192]{0:T(256)} %param.13) | copy-start | bytes 2308
  1.4 1.2 %copy-start.6 = (f32[24]{0:T(128)S(1)}, f32[24]{0:T(128)}, u32[]{:S(2)}) copy-start(f32[24]{0:T(128)} %param.19) | copy-start | bytes 292
  1.4 1.2 %copy-start.7 = (f32[24]{0:T(128)S(1)}, f32[24]{0:T(128)}, u32[]{:S(2)}) copy-start(f32[24]{0:T(128)} %param.20) | copy-start | bytes 292
  1.4 1.2 %copy-start.8 = (f32[24]{0:T(128)S(1)}, f32[24]{0:T(128)}, u32[]{:S(2)}) copy-start(f32[24]{0:T(128)} %param.21) | copy-start | bytes 292
  2.6 1.0 %copy-start.1 = (bf16[192,768]{1,0:T(8,128)(2,1)S(1)}, bf16[192,768]{1,0:T(8,128)(2,1)}, u32[]{:S(2)}) copy-start(bf16[192,768]{1,0:T(8,128)(2,1)} %in_w_ref.1) | copy-start | bytes 884740
  3.6 0.9 %copy-start.2 = (bf16[384,192]{0,1:T(8,128)(2,1)S(1)}, bf16[384,192]{0,1:T(8,128)(2,1)}, u32[]{:S(2)}) copy-start(bf16[384,192]{0,1:T(8,128)(2,1)} %param.23) | copy-start | bytes 442372

commit v3 on v2

--- a/solution.py
+++ b/solution.py
@@ -89,7 +89,7 @@
     c_recv,
 ):
     me = lax.axis_index("seq")
-    tokens, width = region_ref.shape[1], region_ref.shape[2]
+    width, tokens = region_ref.shape
     inner = out_w_ref.shape[1]
     band = tokens // n
     head = inner // heads
@@ -116,7 +116,7 @@
 
     def halo_copy(slot, device):
         return pltpu.make_async_remote_copy(
-            src_ref=region_ref.at[0],
+            src_ref=region_ref,
             dst_ref=halo.at[slot],
             send_sem=halo_send.at[slot],
             recv_sem=halo_recv.at[slot],
@@ -131,15 +131,20 @@
     def _():
         halo_copy(1, me - 1).start()
 
+    square = (width, width)
+    gain_column = jnp.sum(
+        jnp.where(iota(square, 0) == iota(square, 1), norm_gain_ref[...], 0.0), axis=1, keepdims=True
+    )
+
     def normed(values):
-        mean_square = jnp.mean(values * values, axis=-1, keepdims=True)
-        return (values * lax.rsqrt(mean_square + EPSILON) * norm_gain_ref[...]).astype(BF)
+        mean_square = jnp.mean(values * values, axis=0, keepdims=True)
+        return (values * lax.rsqrt(mean_square + EPSILON) * gain_column).astype(BF)
 
     edge = jnp.zeros((8, inner), F32)
     for a in range(3):
         pre[a, 0:8, :] = edge
         pre[a, tokens + 8 : tokens + 16, :] = edge
-    own = mm(normed(region_ref[0].astype(F32)), in_w_ref[...]).astype(BF)
+    own = mm_tn(normed(region_ref[...].astype(F32)), in_w_ref[...]).astype(BF)
     pre[1, 8 : tokens + 8, :] = own[:, :inner].astype(F32)
     gate[...] = own[:, inner:]
 
@@ -150,7 +155,7 @@
 
     @pl.when(me == n - 1)
     def _():
-        halo[1] = jnp.zeros((tokens, width), BF)
+        halo[1] = jnp.zeros((width, tokens), BF)
 
     @pl.when(me > 0)
     def _():
@@ -159,11 +164,20 @@
 
     @pl.when(me == 0)
     def _():
-        halo[0] = jnp.zeros((tokens, width), BF)
+        halo[0] = jnp.zeros((width, tokens), BF)
 
     for slot, a in ((0, 0), (1, 2)):
-        rim = mm(normed(halo[slot].astype(F32)), in_w_ref[:, :inner]).astype(BF)
+        rim = mm_tn(normed(halo[slot].astype(F32)), in_w_ref[:, :inner]).astype(BF)
         pre[a, 8 : tokens + 8, :] = rim.astype(F32)
+
+    def a_copy(k, chunk, place):
+        return pltpu.make_async_remote_copy(
+            src_ref=act.at[chunk],
+            dst_ref=colbuf.at[place],
+            send_sem=a_send.at[k],
+            recv_sem=a_recv.at[k],
+            device_id={"seq": chunk},
+        )
 
     per = TILE // band if band < TILE else 1
     for c in range(tokens // TILE):
@@ -180,15 +194,12 @@
             where = c * TILE // band
             start = c * TILE % band
             act[where, start : start + TILE] = done
-
-    def a_copy(k, chunk, place):
-        return pltpu.make_async_remote_copy(
-            src_ref=act.at[chunk],
-            dst_ref=colbuf.at[place],
-            send_sem=a_send.at[k],
-            recv_sem=a_recv.at[k],
-            device_id={"seq": chunk},
-        )
+        for d in range(c * TILE // band, (c + 1) * TILE // band):
+
+            @pl.when(me != d)
+            def _(d=d):
+                a_copy(lax.rem(d - me + n, n), d, me).start()
+
 
     def s_copy(p, k, chunk, place):
         return pltpu.make_async_remote_copy(
@@ -247,7 +258,6 @@
 
         lax.fori_loop(1, n, one, 0)
 
-    start_all(a_copy)
     colbuf[pl.ds(me, 1)] = act[pl.ds(me, 1)]
 
     group_lane = iota((1, groups), 1)
@@ -296,10 +306,8 @@
             writer = coup[p, :, 2 * o * state : (2 * o + 1) * state]
             contribs.append(mm_tn(writer, weighted))
         for d in range(n):
-            pieces = [v[d * part : (d + 1) * part] for v in contribs]
-            if 2 * part < 16:
-                pieces.append(jnp.zeros((16 - 2 * part, inner), F32))
-            msg[p, d] = jnp.concatenate(pieces, axis=0).astype(BF)
+            for o in range(2):
+                msg[p, d, o * part : (o + 1) * part] = contribs[o][d * part : (d + 1) * part]
         start_all(functools.partial(s_copy, p))
         got[p, pl.ds(me, 1)] = msg[p, pl.ds(me, 1)]
         def diagonal(o):
@@ -358,14 +366,14 @@
         ahead = []
         for i in range(n):
             ahead.append(entry)
-            entry = fade_a[8 * i : 8 * i + 1] * entry + got[p, i].astype(F32)[0:part]
+            entry = fade_a[8 * i : 8 * i + 1] * entry + got[p, i, 0:part, :]
         entry = jnp.zeros((part, inner), F32)
         for i in reversed(range(n)):
             pieces = [ahead[i], entry]
             if 2 * part < 16:
                 pieces.append(jnp.zeros((16 - 2 * part, inner), F32))
             ent_out[p, i] = jnp.concatenate(pieces, axis=0).astype(BF)
-            entry = fade_b[8 * i : 8 * i + 1] * entry + got[p, i].astype(F32)[part : 2 * part]
+            entry = fade_b[8 * i : 8 * i + 1] * entry + got[p, i, part : 2 * part, :]
         start_all(functools.partial(e_copy, p))
         ent_in[p, pl.ds(me, 1)] = ent_out[p, pl.ds(me, 1)]
 
@@ -418,8 +426,8 @@
         gated = (own_row[rows, :] + col.astype(F32)) * own_col[rows, :]
         mean_square = jnp.mean(gated * gated, axis=-1, keepdims=True)
         normy = (gated * lax.rsqrt(mean_square + EPSILON) * out_gain_ref[...]).astype(BF)
-        out_ref[0, rows, :] = (
-            region_ref[0, rows, :].astype(F32) + mm_nt(normy, out_w_ref[...])
+        out_ref[:, rows] = (
+            region_ref[:, rows].astype(F32) + mm_nt(out_w_ref[...], normy)
         ).astype(BF)
     wait_sent(a_copy)
     for p in range(2):
@@ -439,18 +447,19 @@
     band = tokens // n
     part = state // n
     flat = [v if v.ndim > 1 else v.reshape(1, -1) for v in args]
+    flat[0] = region[0].T
     flat[6] = flat[6].T
     flat[11] = flat[11].T
     ent_rows = max(16, 2 * part)
     dma = pltpu.SemaphoreType.DMA
     vmem = pltpu.VMEM
-    return pl.pallas_call(
+    refined = pl.pallas_call(
         functools.partial(kernel, n, heads, state),
-        out_shape=jax.ShapeDtypeStruct(region.shape, BF),
+        out_shape=jax.ShapeDtypeStruct((width, tokens), BF),
         in_specs=[pl.BlockSpec(memory_space=pltpu.VMEM)] * len(flat),
         out_specs=pl.BlockSpec(memory_space=pltpu.VMEM),
         scratch_shapes=[
-            vmem((2, tokens, width), BF),
+            vmem((2, width, tokens), BF),
             vmem((3, tokens + 16, inner), F32),
             vmem((tokens, inner), BF),
             vmem((n, band, inner), BF),
@@ -464,8 +473,8 @@
             vmem((2, groups, tokens), F32),
             vmem((tokens, inner), F32),
             vmem((tokens, inner), F32),
-            vmem((2, n, ent_rows, inner), BF),
-            vmem((2, n, ent_rows, inner), BF),
+            vmem((2, n, 2 * part, inner), F32),
+            vmem((2, n, 2 * part, inner), F32),
             vmem((2, 8, 128), F32),
             vmem((2, n, 8, 128), F32),
             vmem((2, n, ent_rows, inner), BF),
@@ -489,6 +498,7 @@
             collective_id=0, has_side_effects=True, vmem_limit_bytes=50 * 1024 * 1024
         ),
     )(*flat)
+    return refined.T[None]
 
 
 def solution(mesh):

time: 58.4 us -> 60.6 us (1.038)
  local copies, waits for them, and re-layouts: 5.23 us -> 7.29 us
    unnamed x19 -> x21, local copies, waits for them, and re-layouts: 3.01 us -> 5.87 us
    pallas_call x1 -> x0, local copies, waits for them, and re-layouts: 0.8 us -> none  [body(): pl.pallas_call(functools.partial(kernel, n, heads, state), out_shape=jax....]
where the time goes in v3:
time: 60.6 us; the launch traced here: 60.2 us
  Pallas kernels  52.9 us (87%)
  local copies, waits for them, and re-layouts  7.29 us (12%)
    pallas_call x1, Pallas kernels, body(): pl.pallas_call(functools.partial(kernel, n, heads, state), out_shape=jax....  52.9 us
    unnamed x21, local copies, waits for them, and re-layouts  5.87 us
    reshape x2, local copies, waits for them, and re-layouts, body(): flat = [v if v.ndim > 1 else v.reshape(1, -1) for v in args]  1.41 us

profile of v3, /device:TPU:0, one launch (start us, length us, event | category | flops | bytes accessed | tf_op | source)
XLA Modules:
  0.0 60.2 jit_solution(12821692003918642112)
XLA Ops:
  0.0 0.0 copy-start.5
  0.0 0.7 %reshape.19.conv_b_ref = f32[1,384]{1,0:T(1,128)S(1)} reshape(f32[384]{0:T(512)} %param.16) | data formatting | bytes 3072 | tf_op jit(solution)/shard_map/reshape | solution.py:449
  0.7 0.0 copy-start.6
  0.7 0.0 copy-start.7
  0.7 0.0 copy-start.8
  0.7 0.7 %reshape.23.out_gain_ref = f32[1,384]{1,0:T(1,128)S(1)} reshape(f32[384]{0:T(512)} %param.22) | data formatting | bytes 3072 | tf_op jit(solution)/shard_map/reshape | solution.py:449
  1.4 0.0 copy-done.5
  1.4 0.0 copy-done.6
  1.4 0.0 copy-done.7
  1.4 0.0 copy-done.8
  1.4 0.0 copy-start
  1.5 1.0 %copy-done = bf16[384,512]{1,0:T(8,128)(2,1)S(1)} copy-done((bf16[384,512]{1,0:T(8,128)(2,1)S(1)}, bf16[384,512]{1,0:T(8,128)(2,1)}, u32[]{:S(2)}) %copy-start) | copy-done | bytes 393240
  2.4 0.0 copy-start.1
  2.4 1.0 %copy-done.1 = bf16[192,768]{1,0:T(8,128)(2,1)S(1)} copy-done((bf16[192,768]{1,0:T(8,128)(2,1)S(1)}, bf16[192,768]{1,0:T(8,128)(2,1)}, u32[]{:S(2)}) %copy-start.1) | copy-done | bytes 294936
  3.4 0.0 copy-start.2
  3.4 0.9 %copy-done.2 = bf16[1,512,192]{1,2,0:T(8,128)(2,1)S(1)} copy-done((bf16[1,512,192]{1,2,0:T(8,128)(2,1)S(1)}, bf16[1,512,192]{1,2,0:T(8,128)(2,1)}, u32[]{:S(2)}) %copy-start.2) | copy-done | bytes 196632
  4.3 0.0 copy-start.3
  4.3 0.9 %copy-done.3 = bf16[384,192]{0,1:T(8,128)(2,1)S(1)} copy-done((bf16[384,192]{0,1:T(8,128)(2,1)S(1)}, bf16[384,192]{0,1:T(8,128)(2,1)}, u32[]{:S(2)}) %copy-start.3) | copy-done | bytes 147480
  5.2 0.0 copy-start.4
  5.2 0.7 %copy-done.4 = f32[9,384]{1,0:T(8,128)S(1)} copy-done((f32[9,384]{1,0:T(8,128)S(1)}, f32[9,384]{1,0:T(8,128)}, u32[]{:S(2)}) %copy-start.4) | copy-done | bytes 13848
  6.0 0.0 copy-start.9
  6.0 0.7 %copy-done.9 = f32[24]{0:T(128)S(1)} copy-done((f32[24]{0:T(128)S(1)}, f32[24]{0:T(128)}, u32[]{:S(2)}) %copy-start.9) | copy-done | bytes 120
  6.6 52.9 %shard_map.118 = bf16[192,512]{1,0:T(8,128)(2,1)S(1)} custom-call(bf16[192,512]{1,0:T(8,128)(2,1)S(1)} %bitcast.13, f32[1,192]{1,0:T(1,128)S(1)} %bitcast.16, bf16[192,768]{1,0:T(8,128)(2,1)S(1)} %copy-done.1, f32[9,384]{1,0:T(8,128)S(1)} %copy-done.4, f32[1,384]{1,0:T(1,128)S(1)} %reshape.19.conv_b_ref, bf16[384,512]{1,0:T(8,128)(2,1)S(1)} %copy-done, ...), custom_call_target="tpu_custom_call" | custom-call | tf_op jit(solution)/shard_map/pallas_call | solution.py:456
  59.5 0.7 %copy.14 = bf16[1,512,192]{1,2,0:T(8,128)(2,1)} copy(bf16[1,512,192]{1,2,0:T(8,128)(2,1)S(1)} %bitcast.12) | data formatting | bytes 393216
Async XLA Ops:
  0.0 1.4 %copy-start.5 = (bf16[384,24]{0,1:T(8,128)(2,1)S(1)}, bf16[384,24]{0,1:T(8,128)(2,1)}, u32[]{:S(2)}) copy-start(bf16[384,24]{0,1:T(8,128)(2,1)} %param.18) | copy-start | bytes 55300
  0.7 0.7 %copy-start.6 = (f32[192]{0:T(256)S(1)}, f32[192]{0:T(256)}, u32[]{:S(2)}) copy-start(f32[192]{0:T(256)} %param.13) | copy-start | bytes 2308
  0.7 0.7 %copy-start.7 = (f32[24]{0:T(128)S(1)}, f32[24]{0:T(128)}, u32[]{:S(2)}) copy-start(f32[24]{0:T(128)} %param.19) | copy-start | bytes 292
  0.7 0.7 %copy-start.8 = (f32[24]{0:T(128)S(1)}, f32[24]{0:T(128)}, u32[]{:S(2)}) copy-start(f32[24]{0:T(128)} %param.20) | copy-start | bytes 292
  1.4 1.0 %copy-start = (bf16[384,512]{1,0:T(8,128)(2,1)S(1)}, bf16[384,512]{1,0:T(8,128)(2,1)}, u32[]{:S(2)}) copy-start(bf16[384,512]{1,0:T(8,128)(2,1)} %coup_w_ref.1) | copy-start | bytes 1179652
  2.4 1.0 %copy-start.1 = (bf16[192,768]{1,0:T(8,128)(2,1)S(1)}, bf16[192,768]{1,0:T(8,128)(2,1)}, u32[]{:S(2)}) copy-start(bf16[192,768]{1,0:T(8,128)(2,1)} %in_w_ref.1) | copy-start | bytes 884740
  3.4 0.9 %copy-start.2 = (bf16[1,512,192]{1,2,0:T(8,128)(2,1)S(1)}, bf16[1,512,192]{1,2,0:T(8,128)(2,1)}, u32[]{:S(2)}) copy-start(bf16[1,512,192]{1,2,0:T(8,128)(2,1)} %param.12) | copy-start | bytes 589828
  4.3 0.9 %copy-start.3 = (bf16[384,192]{0,1:T(8,128)(2,1)S(1)}, bf16[384,192]{0,1:T(8,128)(2,1)}, u32[]{:S(2)}) copy-start(bf16[384,192]{0,1:T(8,128)(2,1)} %param.23) | copy-start | bytes 442372
  5.2 0.7 %copy-start.4 = (f32[9,384]{1,0:T(8,128)S(1)}, f32[9,384]{1,0:T(8,128)}, u32[]{:S(2)}) copy-start(f32[9,384]{1,0:T(8,128)} %conv_w_ref.1) | copy-start | bytes 41476
  6.0 0.7 %copy-start.9 = (f32[24]{0:T(128)S(1)}, f32[24]{0:T(128)}, u32[]{:S(2)}) copy-start(f32[24]{0:T(128)} %param.21) | copy-start | bytes 292

commit v4 on v3

--- a/solution.py
+++ b/solution.py
@@ -291,8 +291,6 @@
         total = ahead[tokens - 1 : tokens, :]
         c = jnp.where(behind_lane, total - ahead + logs, ahead)
         cum[p] = c
-        cum_t[p] = flip_axes(c)
-        step_t[p] = flip_axes(steps)
         tail = jnp.exp(total - c) * steps
         base = p * 2 * heads
         xf = x.astype(F32)
@@ -308,7 +306,10 @@
         for d in range(n):
             for o in range(2):
                 msg[p, d, o * part : (o + 1) * part] = contribs[o][d * part : (d + 1) * part]
-        start_all(functools.partial(s_copy, p))
+        if p == 1:
+            start_all(functools.partial(s_copy, p))
+        cum_t[p] = flip_axes(c)
+        step_t[p] = flip_axes(steps)
         got[p, pl.ds(me, 1)] = msg[p, pl.ds(me, 1)]
         def diagonal(o):
             w = coup[p, :, 2 * o * state : (2 * o + 1) * state].astype(F32)
@@ -397,14 +398,15 @@
     tiles = tokens // TILE
     mix(0, 0, tiles)
     wait_all(a_copy)
+    start_all(functools.partial(s_copy, 0))
     place = iota((tokens, tokens), 0)
     cell = iota((tokens, tokens), 1)
     turn = cell == jnp.left_shift(jnp.bitwise_and(place, n - 1), band_bits) + jnp.right_shift(place, n_bits)
     xcol[...] = mm(turn.astype(BF), colbuf[...].reshape(tokens, inner)).astype(BF)
     prepare(1, xcol[...])
-    scan(0)
     mix(1, 0, tiles // 2)
     scan(1)
+    scan(0)
     mix(1, tiles // 2, tiles)
     column = finish(1).astype(BF)
     back = cell == jnp.left_shift(jnp.bitwise_and(place, band - 1), n_bits) + jnp.right_shift(place, band_bits)

time: 60.6 us -> 59.8 us (0.987)
  Pallas kernels: 52.9 us -> 52.1 us
    pallas_call x1, Pallas kernels: 52.9 us -> 52.1 us  [body(): pl.pallas_call(functools.partial(kernel, n, heads, state), out_shape=jax....]
where the time goes in v4:
time: 59.8 us; the launch traced here: 59.5 us
  Pallas kernels  52.1 us (87%)
  local copies, waits for them, and re-layouts  7.29 us (12%)
    pallas_call x1, Pallas kernels, body(): pl.pallas_call(functools.partial(kernel, n, heads, state), out_shape=jax....  52.1 us
    unnamed x21, local copies, waits for them, and re-layouts  5.87 us
    reshape x2, local copies, waits for them, and re-layouts, body(): flat = [v if v.ndim > 1 else v.reshape(1, -1) for v in args]  1.41 us

profile of v4, /device:TPU:0, one launch (start us, length us, event | category | flops | bytes accessed | tf_op | source)
XLA Modules:
  0.0 59.5 jit_solution(14377518763146827077)
XLA Ops:
  0.0 0.0 copy-start.5
  0.0 0.7 %reshape.19.conv_b_ref = f32[1,384]{1,0:T(1,128)S(1)} reshape(f32[384]{0:T(512)} %param.16) | data formatting | bytes 3072 | tf_op jit(solution)/shard_map/reshape | solution.py:451
  0.7 0.0 copy-start.6
  0.7 0.0 copy-start.7
  0.7 0.0 copy-start.8
  0.7 0.7 %reshape.23.out_gain_ref = f32[1,384]{1,0:T(1,128)S(1)} reshape(f32[384]{0:T(512)} %param.22) | data formatting | bytes 3072 | tf_op jit(solution)/shard_map/reshape | solution.py:451
  1.4 0.0 copy-done.5
  1.4 0.0 copy-done.6
  1.4 0.0 copy-done.7
  1.4 0.0 copy-done.8
  1.4 0.0 copy-start
  1.5 1.0 %copy-done = bf16[384,512]{1,0:T(8,128)(2,1)S(1)} copy-done((bf16[384,512]{1,0:T(8,128)(2,1)S(1)}, bf16[384,512]{1,0:T(8,128)(2,1)}, u32[]{:S(2)}) %copy-start) | copy-done | bytes 393240
  2.4 0.0 copy-start.1
  2.4 1.0 %copy-done.1 = bf16[192,768]{1,0:T(8,128)(2,1)S(1)} copy-done((bf16[192,768]{1,0:T(8,128)(2,1)S(1)}, bf16[192,768]{1,0:T(8,128)(2,1)}, u32[]{:S(2)}) %copy-start.1) | copy-done | bytes 294936
  3.4 0.0 copy-start.2
  3.4 0.9 %copy-done.2 = bf16[1,512,192]{1,2,0:T(8,128)(2,1)S(1)} copy-done((bf16[1,512,192]{1,2,0:T(8,128)(2,1)S(1)}, bf16[1,512,192]{1,2,0:T(8,128)(2,1)}, u32[]{:S(2)}) %copy-start.2) | copy-done | bytes 196632
  4.3 0.0 copy-start.3
  4.3 0.9 %copy-done.3 = bf16[384,192]{0,1:T(8,128)(2,1)S(1)} copy-done((bf16[384,192]{0,1:T(8,128)(2,1)S(1)}, bf16[384,192]{0,1:T(8,128)(2,1)}, u32[]{:S(2)}) %copy-start.3) | copy-done | bytes 147480
  5.2 0.0 copy-start.4
  5.2 0.7 %copy-done.4 = f32[9,384]{1,0:T(8,128)S(1)} copy-done((f32[9,384]{1,0:T(8,128)S(1)}, f32[9,384]{1,0:T(8,128)}, u32[]{:S(2)}) %copy-start.4) | copy-done | bytes 13848
  6.0 0.0 copy-start.9
  6.0 0.7 %copy-done.9 = f32[24]{0:T(128)S(1)} copy-done((f32[24]{0:T(128)S(1)}, f32[24]{0:T(128)}, u32[]{:S(2)}) %copy-start.9) | copy-done | bytes 120
  6.6 52.1 %shard_map.118 = bf16[192,512]{1,0:T(8,128)(2,1)S(1)} custom-call(bf16[192,512]{1,0:T(8,128)(2,1)S(1)} %bitcast.13, f32[1,192]{1,0:T(1,128)S(1)} %bitcast.16, bf16[192,768]{1,0:T(8,128)(2,1)S(1)} %copy-done.1, f32[9,384]{1,0:T(8,128)S(1)} %copy-done.4, f32[1,384]{1,0:T(1,128)S(1)} %reshape.19.conv_b_ref, bf16[384,512]{1,0:T(8,128)(2,1)S(1)} %copy-done, ...), custom_call_target="tpu_custom_call" | custom-call | tf_op jit(solution)/shard_map/pallas_call | solution.py:458
  58.8 0.7 %copy.14 = bf16[1,512,192]{1,2,0:T(8,128)(2,1)} copy(bf16[1,512,192]{1,2,0:T(8,128)(2,1)S(1)} %bitcast.12) | data formatting | bytes 393216
Async XLA Ops:
  0.0 1.4 %copy-start.5 = (bf16[384,24]{0,1:T(8,128)(2,1)S(1)}, bf16[384,24]{0,1:T(8,128)(2,1)}, u32[]{:S(2)}) copy-start(bf16[384,24]{0,1:T(8,128)(2,1)} %param.18) | copy-start | bytes 55300
  0.7 0.7 %copy-start.6 = (f32[192]{0:T(256)S(1)}, f32[192]{0:T(256)}, u32[]{:S(2)}) copy-start(f32[192]{0:T(256)} %param.13) | copy-start | bytes 2308
  0.7 0.7 %copy-start.7 = (f32[24]{0:T(128)S(1)}, f32[24]{0:T(128)}, u32[]{:S(2)}) copy-start(f32[24]{0:T(128)} %param.19) | copy-start | bytes 292
  0.7 0.7 %copy-start.8 = (f32[24]{0:T(128)S(1)}, f32[24]{0:T(128)}, u32[]{:S(2)}) copy-start(f32[24]{0:T(128)} %param.20) | copy-start | bytes 292
  1.4 1.0 %copy-start = (bf16[384,512]{1,0:T(8,128)(2,1)S(1)}, bf16[384,512]{1,0:T(8,128)(2,1)}, u32[]{:S(2)}) copy-start(bf16[384,512]{1,0:T(8,128)(2,1)} %coup_w_ref.1) | copy-start | bytes 1179652
  2.4 1.0 %copy-start.1 = (bf16[192,768]{1,0:T(8,128)(2,1)S(1)}, bf16[192,768]{1,0:T(8,128)(2,1)}, u32[]{:S(2)}) copy-start(bf16[192,768]{1,0:T(8,128)(2,1)} %in_w_ref.1) | copy-start | bytes 884740
  3.4 0.9 %copy-start.2 = (bf16[1,512,192]{1,2,0:T(8,128)(2,1)S(1)}, bf16[1,512,192]{1,2,0:T(8,128)(2,1)}, u32[]{:S(2)}) copy-start(bf16[1,512,192]{1,2,0:T(8,128)(2,1)} %param.12) | copy-start | bytes 589828
  4.3 0.9 %copy-start.3 = (bf16[384,192]{0,1:T(8,128)(2,1)S(1)}, bf16[384,192]{0,1:T(8,128)(2,1)}, u32[]{:S(2)}) copy-start(bf16[384,192]{0,1:T(8,128)(2,1)} %param.23) | copy-start | bytes 442372
  5.2 0.7 %copy-start.4 = (f32[9,384]{1,0:T(8,128)S(1)}, f32[9,384]{1,0:T(8,128)}, u32[]{:S(2)}) copy-start(f32[9,384]{1,0:T(8,128)} %conv_w_ref.1) | copy-start | bytes 41476
  6.0 0.7 %copy-start.9 = (f32[24]{0:T(128)S(1)}, f32[24]{0:T(128)}, u32[]{:S(2)}) copy-start(f32[24]{0:T(128)} %param.21) | copy-start | bytes 292

commit v5 on v4

--- a/solution.py
+++ b/solution.py
@@ -114,22 +114,35 @@
     lax.fori_loop(1, n, greet, 0)
     pl.semaphore_wait(barrier, n - 1)
 
-    def halo_copy(slot, device):
+    tiles = tokens // TILE
+
+    def halo_copy(slot, c, device):
+        cells = pl.ds(c * TILE, TILE)
         return pltpu.make_async_remote_copy(
-            src_ref=region_ref,
-            dst_ref=halo.at[slot],
-            send_sem=halo_send.at[slot],
-            recv_sem=halo_recv.at[slot],
+            src_ref=region_ref.at[:, cells],
+            dst_ref=halo.at[slot, :, cells],
+            send_sem=halo_send.at[slot, c],
+            recv_sem=halo_recv.at[slot, c],
             device_id={"seq": device},
         )
 
-    @pl.when(me < n - 1)
+    for c in range(tiles):
+
+        @pl.when(me < n - 1)
+        def _(c=c):
+            halo_copy(0, c, me + 1).start()
+
+        @pl.when(me > 0)
+        def _(c=c):
+            halo_copy(1, c, me - 1).start()
+
+    @pl.when(me == n - 1)
     def _():
-        halo_copy(0, me + 1).start()
-
-    @pl.when(me > 0)
+        halo[1] = jnp.zeros((width, tokens), BF)
+
+    @pl.when(me == 0)
     def _():
-        halo_copy(1, me - 1).start()
+        halo[0] = jnp.zeros((width, tokens), BF)
 
     square = (width, width)
     gain_column = jnp.sum(
@@ -144,31 +157,8 @@
     for a in range(3):
         pre[a, 0:8, :] = edge
         pre[a, tokens + 8 : tokens + 16, :] = edge
-    own = mm_tn(normed(region_ref[...].astype(F32)), in_w_ref[...]).astype(BF)
-    pre[1, 8 : tokens + 8, :] = own[:, :inner].astype(F32)
-    gate[...] = own[:, inner:]
-
-    @pl.when(me < n - 1)
-    def _():
-        halo_copy(1, me + 1).wait_recv()
-        halo_copy(0, me + 1).wait_send()
-
-    @pl.when(me == n - 1)
-    def _():
-        halo[1] = jnp.zeros((width, tokens), BF)
-
-    @pl.when(me > 0)
-    def _():
-        halo_copy(0, me - 1).wait_recv()
-        halo_copy(1, me - 1).wait_send()
-
-    @pl.when(me == 0)
-    def _():
-        halo[0] = jnp.zeros((width, tokens), BF)
-
-    for slot, a in ((0, 0), (1, 2)):
-        rim = mm_tn(normed(halo[slot].astype(F32)), in_w_ref[:, :inner]).astype(BF)
-        pre[a, 8 : tokens + 8, :] = rim.astype(F32)
+    own = normed(region_ref[...].astype(F32))
+    pre[1, 8 : tokens + 8, :] = mm_tn(own, in_w_ref[:, :inner]).astype(BF).astype(F32)
 
     def a_copy(k, chunk, place):
         return pltpu.make_async_remote_copy(
@@ -180,7 +170,7 @@
         )
 
     per = TILE // band if band < TILE else 1
-    for c in range(tokens // TILE):
+    def convolve(c):
         summed = conv_b_ref[...]
         for a in range(3):
             for b in range(3):
@@ -200,6 +190,26 @@
             def _(d=d):
                 a_copy(lax.rem(d - me + n, n), d, me).start()
 
+
+    for c in range(tiles + 1):
+        if c < tiles:
+
+            @pl.when(me < n - 1)
+            def _(c=c):
+                halo_copy(1, c, me + 1).wait_recv()
+
+            @pl.when(me > 0)
+            def _(c=c):
+                halo_copy(0, c, me - 1).wait_recv()
+
+            cells = slice(c * TILE, (c + 1) * TILE)
+            for slot, a in ((0, 0), (1, 2)):
+                rim = mm_tn(normed(halo[slot, :, cells].astype(F32)), in_w_ref[:, :inner])
+                pre[a, 8 + c * TILE : 8 + (c + 1) * TILE, :] = rim.astype(BF).astype(F32)
+        if c > 0:
+            convolve(c - 1)
+
+    gate[...] = mm_tn(own, in_w_ref[:, inner:]).astype(BF)
 
     def s_copy(p, k, chunk, place):
         return pltpu.make_async_remote_copy(
@@ -395,7 +405,6 @@
 
     x_row = act[...].reshape(tokens, inner)
     prepare(0, x_row)
-    tiles = tokens // TILE
     mix(0, 0, tiles)
     wait_all(a_copy)
     start_all(functools.partial(s_copy, 0))
@@ -431,6 +440,16 @@
         out_ref[:, rows] = (
             region_ref[:, rows].astype(F32) + mm_nt(out_w_ref[...], normy)
         ).astype(BF)
+    for c in range(tiles):
+
+        @pl.when(me < n - 1)
+        def _(c=c):
+            halo_copy(0, c, me + 1).wait_send()
+
+        @pl.when(me > 0)
+        def _(c=c):
+            halo_copy(1, c, me - 1).wait_send()
+
     wait_sent(a_copy)
     for p in range(2):
         wait_sent(functools.partial(s_copy, p))
@@ -483,8 +502,8 @@
             vmem((2, n, ent_rows, inner), BF),
             vmem((n, band, inner), BF),
             vmem((n, band, inner), BF),
-            dma((2,)),
-            dma((2,)),
+            dma((2, tokens // TILE)),
+            dma((2, tokens // TILE)),
             dma((n,)),
             dma((n,)),
             dma((2, n)),

time: 59.8 us -> 59.9 us (level)
  no operation moved by 1% of the time
where the time goes in v5:
time: 59.9 us; the launch traced here: 59.5 us
  Pallas kernels  52.2 us (87%)
  local copies, waits for them, and re-layouts  7.29 us (12%)
    pallas_call x1, Pallas kernels, body(): pl.pallas_call(functools.partial(kernel, n, heads, state), out_shape=jax....  52.2 us
    unnamed x21, local copies, waits for them, and re-layouts  5.87 us
    reshape x2, local copies, waits for them, and re-layouts, body(): flat = [v if v.ndim > 1 else v.reshape(1, -1) for v in args]  1.41 us

profile of v5, /device:TPU:0, one launch (start us, length us, event | category | flops | bytes accessed | tf_op | source)
XLA Modules:
  0.0 59.5 jit_solution(6161011672347512094)
XLA Ops:
  0.0 0.0 copy-start.5
  0.0 0.7 %reshape.19.conv_b_ref = f32[1,384]{1,0:T(1,128)S(1)} reshape(f32[384]{0:T(512)} %param.16) | data formatting | bytes 3072 | tf_op jit(solution)/shard_map/reshape | solution.py:470
  0.7 0.0 copy-start.6
  0.7 0.0 copy-start.7
  0.7 0.0 copy-start.8
  0.7 0.7 %reshape.23.out_gain_ref = f32[1,384]{1,0:T(1,128)S(1)} reshape(f32[384]{0:T(512)} %param.22) | data formatting | bytes 3072 | tf_op jit(solution)/shard_map/reshape | solution.py:470
  1.4 0.0 copy-done.5
  1.4 0.0 copy-done.6
  1.4 0.0 copy-done.7
  1.4 0.0 copy-done.8
  1.4 0.0 copy-start
  1.5 1.0 %copy-done = bf16[384,512]{1,0:T(8,128)(2,1)S(1)} copy-done((bf16[384,512]{1,0:T(8,128)(2,1)S(1)}, bf16[384,512]{1,0:T(8,128)(2,1)}, u32[]{:S(2)}) %copy-start) | copy-done | bytes 393240
  2.4 0.0 copy-start.1
  2.4 1.0 %copy-done.1 = bf16[192,768]{1,0:T(8,128)(2,1)S(1)} copy-done((bf16[192,768]{1,0:T(8,128)(2,1)S(1)}, bf16[192,768]{1,0:T(8,128)(2,1)}, u32[]{:S(2)}) %copy-start.1) | copy-done | bytes 294936
  3.4 0.0 copy-start.2
  3.4 0.9 %copy-done.2 = bf16[1,512,192]{1,2,0:T(8,128)(2,1)S(1)} copy-done((bf16[1,512,192]{1,2,0:T(8,128)(2,1)S(1)}, bf16[1,512,192]{1,2,0:T(8,128)(2,1)}, u32[]{:S(2)}) %copy-start.2) | copy-done | bytes 196632
  4.3 0.0 copy-start.3
  4.3 0.9 %copy-done.3 = bf16[384,192]{0,1:T(8,128)(2,1)S(1)} copy-done((bf16[384,192]{0,1:T(8,128)(2,1)S(1)}, bf16[384,192]{0,1:T(8,128)(2,1)}, u32[]{:S(2)}) %copy-start.3) | copy-done | bytes 147480
  5.2 0.0 copy-start.4
  5.2 0.7 %copy-done.4 = f32[9,384]{1,0:T(8,128)S(1)} copy-done((f32[9,384]{1,0:T(8,128)S(1)}, f32[9,384]{1,0:T(8,128)}, u32[]{:S(2)}) %copy-start.4) | copy-done | bytes 13848
  6.0 0.0 copy-start.9
  6.0 0.7 %copy-done.9 = f32[24]{0:T(128)S(1)} copy-done((f32[24]{0:T(128)S(1)}, f32[24]{0:T(128)}, u32[]{:S(2)}) %copy-start.9) | copy-done | bytes 120
  6.6 52.2 %shard_map.118 = bf16[192,512]{1,0:T(8,128)(2,1)S(1)} custom-call(bf16[192,512]{1,0:T(8,128)(2,1)S(1)} %bitcast.13, f32[1,192]{1,0:T(1,128)S(1)} %bitcast.16, bf16[192,768]{1,0:T(8,128)(2,1)S(1)} %copy-done.1, f32[9,384]{1,0:T(8,128)S(1)} %copy-done.4, f32[1,384]{1,0:T(1,128)S(1)} %reshape.19.conv_b_ref, bf16[384,512]{1,0:T(8,128)(2,1)S(1)} %copy-done, ...), custom_call_target="tpu_custom_call" | custom-call | tf_op jit(solution)/shard_map/pallas_call | solution.py:477
  58.8 0.7 %copy.14 = bf16[1,512,192]{1,2,0:T(8,128)(2,1)} copy(bf16[1,512,192]{1,2,0:T(8,128)(2,1)S(1)} %bitcast.12) | data formatting | bytes 393216
Async XLA Ops:
  0.0 1.4 %copy-start.5 = (bf16[384,24]{0,1:T(8,128)(2,1)S(1)}, bf16[384,24]{0,1:T(8,128)(2,1)}, u32[]{:S(2)}) copy-start(bf16[384,24]{0,1:T(8,128)(2,1)} %param.18) | copy-start | bytes 55300
  0.7 0.7 %copy-start.6 = (f32[192]{0:T(256)S(1)}, f32[192]{0:T(256)}, u32[]{:S(2)}) copy-start(f32[192]{0:T(256)} %param.13) | copy-start | bytes 2308
  0.7 0.7 %copy-start.7 = (f32[24]{0:T(128)S(1)}, f32[24]{0:T(128)}, u32[]{:S(2)}) copy-start(f32[24]{0:T(128)} %param.19) | copy-start | bytes 292
  0.7 0.7 %copy-start.8 = (f32[24]{0:T(128)S(1)}, f32[24]{0:T(128)}, u32[]{:S(2)}) copy-start(f32[24]{0:T(128)} %param.20) | copy-start | bytes 292
  1.4 1.0 %copy-start = (bf16[384,512]{1,0:T(8,128)(2,1)S(1)}, bf16[384,512]{1,0:T(8,128)(2,1)}, u32[]{:S(2)}) copy-start(bf16[384,512]{1,0:T(8,128)(2,1)} %coup_w_ref.1) | copy-start | bytes 1179652
  2.4 1.0 %copy-start.1 = (bf16[192,768]{1,0:T(8,128)(2,1)S(1)}, bf16[192,768]{1,0:T(8,128)(2,1)}, u32[]{:S(2)}) copy-start(bf16[192,768]{1,0:T(8,128)(2,1)} %in_w_ref.1) | copy-start | bytes 884740
  3.4 0.9 %copy-start.2 = (bf16[1,512,192]{1,2,0:T(8,128)(2,1)S(1)}, bf16[1,512,192]{1,2,0:T(8,128)(2,1)}, u32[]{:S(2)}) copy-start(bf16[1,512,192]{1,2,0:T(8,128)(2,1)} %param.12) | copy-start | bytes 589828
  4.3 0.9 %copy-start.3 = (bf16[384,192]{0,1:T(8,128)(2,1)S(1)}, bf16[384,192]{0,1:T(8,128)(2,1)}, u32[]{:S(2)}) copy-start(bf16[384,192]{0,1:T(8,128)(2,1)} %param.23) | copy-start | bytes 442372
  5.2 0.7 %copy-start.4 = (f32[9,384]{1,0:T(8,128)S(1)}, f32[9,384]{1,0:T(8,128)}, u32[]{:S(2)}) copy-start(f32[9,384]{1,0:T(8,128)} %conv_w_ref.1) | copy-start | bytes 41476
  6.0 0.7 %copy-start.9 = (f32[24]{0:T(128)S(1)}, f32[24]{0:T(128)}, u32[]{:S(2)}) copy-start(f32[24]{0:T(128)} %param.21) | copy-start | bytes 292

commit v6 on v5

--- a/solution.py
+++ b/solution.py
@@ -419,8 +419,14 @@
     mix(1, tiles // 2, tiles)
     column = finish(1).astype(BF)
     back = cell == jnp.left_shift(jnp.bitwise_and(place, band - 1), n_bits) + jnp.right_shift(place, band_bits)
-    col_out[...] = mm(back.astype(BF), column).astype(BF).reshape(n, band, inner)
-    start_all(c_copy)
+    back = back.astype(BF)
+    for d in range(n):
+        col_out[d] = mm(back[d * band : (d + 1) * band], column).astype(BF)
+
+        @pl.when(me != d)
+        def _(d=d):
+            c_copy(lax.rem(d - me + n, n), d, me).start()
+
     col_in[pl.ds(me, 1)] = col_out[pl.ds(me, 1)]
     row_total = finish(0)
     g = gate[...].astype(F32)

time: 59.9 us -> 59.7 us (level)
  no operation moved by 1% of the time
where the time goes in v6:
time: 59.7 us; the launch traced here: 59.3 us
  Pallas kernels  52 us (87%)
  local copies, waits for them, and re-layouts  7.29 us (12%)
    pallas_call x1, Pallas kernels, body(): pl.pallas_call(functools.partial(kernel, n, heads, state), out_shape=jax....  52 us
    unnamed x21, local copies, waits for them, and re-layouts  5.87 us
    reshape x2, local copies, waits for them, and re-layouts, body(): flat = [v if v.ndim > 1 else v.reshape(1, -1) for v in args]  1.41 us

profile of v6, /device:TPU:0, one launch (start us, length us, event | category | flops | bytes accessed | tf_op | source)
XLA Modules:
  0.0 59.3 jit_solution(1954951672925864046)
XLA Ops:
  0.0 0.0 copy-start.5
  0.0 0.7 %reshape.19.conv_b_ref = f32[1,384]{1,0:T(1,128)S(1)} reshape(f32[384]{0:T(512)} %param.16) | data formatting | bytes 3072 | tf_op jit(solution)/shard_map/reshape | solution.py:476
  0.7 0.0 copy-start.6
  0.7 0.0 copy-start.7
  0.7 0.0 copy-start.8
  0.7 0.7 %reshape.23.out_gain_ref = f32[1,384]{1,0:T(1,128)S(1)} reshape(f32[384]{0:T(512)} %param.22) | data formatting | bytes 3072 | tf_op jit(solution)/shard_map/reshape | solution.py:476
  1.4 0.0 copy-done.5
  1.4 0.0 copy-done.6
  1.4 0.0 copy-done.7
  1.4 0.0 copy-done.8
  1.4 0.0 copy-start
  1.5 1.0 %copy-done = bf16[384,512]{1,0:T(8,128)(2,1)S(1)} copy-done((bf16[384,512]{1,0:T(8,128)(2,1)S(1)}, bf16[384,512]{1,0:T(8,128)(2,1)}, u32[]{:S(2)}) %copy-start) | copy-done | bytes 393240
  2.4 0.0 copy-start.1
  2.4 1.0 %copy-done.1 = bf16[192,768]{1,0:T(8,128)(2,1)S(1)} copy-done((bf16[192,768]{1,0:T(8,128)(2,1)S(1)}, bf16[192,768]{1,0:T(8,128)(2,1)}, u32[]{:S(2)}) %copy-start.1) | copy-done | bytes 294936
  3.4 0.0 copy-start.2
  3.4 0.9 %copy-done.2 = bf16[1,512,192]{1,2,0:T(8,128)(2,1)S(1)} copy-done((bf16[1,512,192]{1,2,0:T(8,128)(2,1)S(1)}, bf16[1,512,192]{1,2,0:T(8,128)(2,1)}, u32[]{:S(2)}) %copy-start.2) | copy-done | bytes 196632
  4.3 0.0 copy-start.3
  4.3 0.9 %copy-done.3 = bf16[384,192]{0,1:T(8,128)(2,1)S(1)} copy-done((bf16[384,192]{0,1:T(8,128)(2,1)S(1)}, bf16[384,192]{0,1:T(8,128)(2,1)}, u32[]{:S(2)}) %copy-start.3) | copy-done | bytes 147480
  5.2 0.0 copy-start.4
  5.2 0.7 %copy-done.4 = f32[9,384]{1,0:T(8,128)S(1)} copy-done((f32[9,384]{1,0:T(8,128)S(1)}, f32[9,384]{1,0:T(8,128)}, u32[]{:S(2)}) %copy-start.4) | copy-done | bytes 13848
  6.0 0.0 copy-start.9
  6.0 0.7 %copy-done.9 = f32[24]{0:T(128)S(1)} copy-done((f32[24]{0:T(128)S(1)}, f32[24]{0:T(128)}, u32[]{:S(2)}) %copy-start.9) | copy-done | bytes 120
  6.6 52.0 %shard_map.118 = bf16[192,512]{1,0:T(8,128)(2,1)S(1)} custom-call(bf16[192,512]{1,0:T(8,128)(2,1)S(1)} %bitcast.13, f32[1,192]{1,0:T(1,128)S(1)} %bitcast.16, bf16[192,768]{1,0:T(8,128)(2,1)S(1)} %copy-done.1, f32[9,384]{1,0:T(8,128)S(1)} %copy-done.4, f32[1,384]{1,0:T(1,128)S(1)} %reshape.19.conv_b_ref, bf16[384,512]{1,0:T(8,128)(2,1)S(1)} %copy-done, ...), custom_call_target="tpu_custom_call" | custom-call | tf_op jit(solution)/shard_map/pallas_call | solution.py:483
  58.6 0.7 %copy.14 = bf16[1,512,192]{1,2,0:T(8,128)(2,1)} copy(bf16[1,512,192]{1,2,0:T(8,128)(2,1)S(1)} %bitcast.12) | data formatting | bytes 393216
Async XLA Ops:
  0.0 1.4 %copy-start.5 = (bf16[384,24]{0,1:T(8,128)(2,1)S(1)}, bf16[384,24]{0,1:T(8,128)(2,1)}, u32[]{:S(2)}) copy-start(bf16[384,24]{0,1:T(8,128)(2,1)} %param.18) | copy-start | bytes 55300
  0.7 0.7 %copy-start.6 = (f32[192]{0:T(256)S(1)}, f32[192]{0:T(256)}, u32[]{:S(2)}) copy-start(f32[192]{0:T(256)} %param.13) | copy-start | bytes 2308
  0.7 0.7 %copy-start.7 = (f32[24]{0:T(128)S(1)}, f32[24]{0:T(128)}, u32[]{:S(2)}) copy-start(f32[24]{0:T(128)} %param.19) | copy-start | bytes 292
  0.7 0.7 %copy-start.8 = (f32[24]{0:T(128)S(1)}, f32[24]{0:T(128)}, u32[]{:S(2)}) copy-start(f32[24]{0:T(128)} %param.20) | copy-start | bytes 292
  1.4 1.0 %copy-start = (bf16[384,512]{1,0:T(8,128)(2,1)S(1)}, bf16[384,512]{1,0:T(8,128)(2,1)}, u32[]{:S(2)}) copy-start(bf16[384,512]{1,0:T(8,128)(2,1)} %coup_w_ref.1) | copy-start | bytes 1179652
  2.4 1.0 %copy-start.1 = (bf16[192,768]{1,0:T(8,128)(2,1)S(1)}, bf16[192,768]{1,0:T(8,128)(2,1)}, u32[]{:S(2)}) copy-start(bf16[192,768]{1,0:T(8,128)(2,1)} %in_w_ref.1) | copy-start | bytes 884740
  3.4 0.9 %copy-start.2 = (bf16[1,512,192]{1,2,0:T(8,128)(2,1)S(1)}, bf16[1,512,192]{1,2,0:T(8,128)(2,1)}, u32[]{:S(2)}) copy-start(bf16[1,512,192]{1,2,0:T(8,128)(2,1)} %param.12) | copy-start | bytes 589828
  4.3 0.9 %copy-start.3 = (bf16[384,192]{0,1:T(8,128)(2,1)S(1)}, bf16[384,192]{0,1:T(8,128)(2,1)}, u32[]{:S(2)}) copy-start(bf16[384,192]{0,1:T(8,128)(2,1)} %param.23) | copy-start | bytes 442372
  5.2 0.7 %copy-start.4 = (f32[9,384]{1,0:T(8,128)S(1)}, f32[9,384]{1,0:T(8,128)}, u32[]{:S(2)}) copy-start(f32[9,384]{1,0:T(8,128)} %conv_w_ref.1) | copy-start | bytes 41476
  6.0 0.7 %copy-start.9 = (f32[24]{0:T(128)S(1)}, f32[24]{0:T(128)}, u32[]{:S(2)}) copy-start(f32[24]{0:T(128)} %param.21) | copy-start | bytes 292
